TPU v7x, 256 devices: a whole 4x4x8 slice. The times are simulated.
256 devices in a mesh: ta: 4 (over y_hi, core), gz: 8 (over z), xy: 8 (over x, y_lo).
Axes of the slice: x: 4, y: 4 (y_hi: 2, y_lo: 2; y = y_hi * 2 + y_lo), z: 8, core: 2. Of those that a mesh axis runs over, the one named last changes fastest.
Arguments:
- fine_source: bfloat16 [4, 32, 8, 8, 2, 2, 2, 1536], P(None, 'ta', 'gz', 'xy'), may hold values from -4 to 4, as said below
- vectors: bfloat16 [32, 8, 8, 2, 2, 2, 32, 1536], P('ta', 'gz', 'xy'), may hold values from -0.75 to 0.75
- coarse_links: bfloat16 [32, 8, 8, 2, 9, 128, 128], P(('ta', 'xy'), 'gz'), may hold values from -1 to 1, as said below
Outputs:
- correction: bfloat16 [4, 32, 8, 8, 2, 2, 2, 1536], P(None, 'ta', 'gz', 'xy')
- coarse_residual: float32 [4, 32, 8, 8, 2, 128], P(None, 'ta', 'gz', 'xy')
Inputs may be any that keep to these rules, and one draw needn't show every extreme that they name: `fine_source`: fine residuals of magnitude at most 4. `coarse_links`: operator block entries of magnitude at most 1.
All inputs are finite; a program needn't handle non-finite values.
Results may differ from a plain program's by a relative error of at most 0.011.
Values may be sent and summed in bfloat16 or wider, within the bound.
No kernel may reach another device: no remote copies, remote signals or barrier semaphores. Data moves between devices by JAX's collectives and lax.ppermute only.
A program may use at most 64 MiB of HBM per device.

v0:
```python
import jax
import jax.numpy as jnp
from jax import lax
from jax.sharding import PartitionSpec as P


def padded_2(array, sides, width):
    for axis, dim in sides:
        devices, length = (lax.axis_size(axis), array.shape[dim])
        up = [(i, (i + 1) % devices) for i in range(devices)]
        down = [(j, i) for i, j in up]
        last = lax.slice_in_dim(array, length - width, length, axis=dim)
        initial = lax.slice_in_dim(array, 0, width, axis=dim)
        before = lax.ppermute(last, axis, up)
        after = lax.ppermute(initial, axis, down)
        array = jnp.concatenate([before, array, after], axis=dim)
    return array


def restrict(fields, vectors):
    real_part = fields[..., 0, :]
    imag_part = fields[..., 1, :]
    turned = jnp.stack([imag_part, -real_part], axis=-2)
    stacked = jnp.stack([fields, turned], axis=-3)
    coarse = jnp.einsum(
        "tzxycpki,rtzxycqpi->rtzxycqk", vectors, stacked, preferred_element_type=jnp.float32
    )
    return coarse.reshape(coarse.shape[:5] + (-1,))


def prolong(solution, vectors):
    parts = solution.reshape(solution.shape[:5] + (2, 2, -1))
    real_part = parts[..., 0, :]
    imag_part = parts[..., 1, :]
    leading = jnp.stack([real_part, -imag_part], axis=-2)
    trailing = jnp.stack([imag_part, real_part], axis=-2)
    stacked = jnp.stack([leading, trailing], axis=-3)
    fields = jnp.einsum(
        "tzxycpki,rtzxycqpk->rtzxycqi", vectors, stacked, preferred_element_type=jnp.float32
    )
    return fields.astype(jnp.bfloat16)


def combine(
    center, plus_time, minus_time, plus_depth, minus_depth, plus_across, minus_across, coarse_links
):
    plus_along = jnp.roll(center, -1, 4)
    minus_along = jnp.roll(center, 1, 4)
    stacked = jnp.stack(
        [
            center,
            -plus_time,
            -minus_time,
            -plus_depth,
            -minus_depth,
            -plus_across,
            -minus_across,
            -plus_along,
            -minus_along,
        ],
        axis=5,
    )
    hops = jnp.einsum(
        "tzxydab,rtzxydb->rtzxya", coarse_links, stacked, preferred_element_type=jnp.float32
    )
    return 4.0 * center.astype(jnp.float32) + hops


def fine_operate(vector, coarse_links):
    center = vector.astype(jnp.bfloat16)
    padded = padded_2(center, (("ta", 1), ("gz", 2), ("xy", 3)), 1)
    return combine(
        center,
        padded[:, 2:, 1:-1, 1:-1],
        padded[:, :-2, 1:-1, 1:-1],
        padded[:, 1:-1, 2:, 1:-1],
        padded[:, 1:-1, :-2, 1:-1],
        padded[:, 1:-1, 1:-1, 2:],
        padded[:, 1:-1, 1:-1, :-2],
        coarse_links,
    )


def dotted(left, right):
    return jnp.sum(left * right, axis=(1, 2, 3, 4, 5))


def spread(values):
    return values.reshape((-1, 1, 1, 1, 1, 1))


def body(fine_source, vectors, coarse_links):
    coarse_rhs = restrict(fine_source, vectors)
    operator_blocks = lax.all_to_all(coarse_links, "xy", split_axis=2, concat_axis=0, tiled=True)
    image_zero = fine_operate(coarse_rhs, operator_blocks)
    norm_zero, correlation_zero = lax.psum(
        (dotted(image_zero, image_zero), dotted(image_zero, coarse_rhs)), ("ta", "gz", "xy")
    )
    alpha_zero = correlation_zero / norm_zero
    iterate_one = spread(alpha_zero) * coarse_rhs
    resid_one = coarse_rhs - spread(alpha_zero) * image_zero
    image_one = fine_operate(resid_one, operator_blocks)
    coupling = lax.psum(dotted(image_zero, image_one), ("ta", "gz", "xy"))
    beta_coef = coupling / norm_zero
    direction = resid_one - spread(beta_coef) * coarse_rhs
    image_one = image_one - spread(beta_coef) * image_zero
    norm_one, correlation_one = lax.psum(
        (dotted(image_one, image_one), dotted(image_one, resid_one)), ("ta", "gz", "xy")
    )
    alpha_one = correlation_one / norm_one
    iterate_two = iterate_one + spread(alpha_one) * direction
    coarse_residual = resid_one - spread(alpha_one) * image_one
    correction = prolong(iterate_two.astype(jnp.bfloat16), vectors)
    return (correction, coarse_residual)


def solution(mesh):
    return jax.shard_map(
        body,
        mesh=mesh,
        in_specs=(
            P(None, "ta", "gz", "xy", None, None, None, None),
            P("ta", "gz", "xy", None, None, None, None, None),
            P(("ta", "xy"), "gz", None, None, None, None, None),
        ),
        out_specs=(
            P(None, "ta", "gz", "xy", None, None, None, None),
            P(None, "ta", "gz", "xy", None, None),
        ),
        check_vma=False,
    )
```

profile of v0, /device:TPU:1, one launch (start us, length us, event | category | flops | bytes accessed | tf_op | source)
XLA Modules:
  0.0 334.6 jit_solution(8173131926435096774)
XLA Ops:
  0.6 0.0 copy-start
  0.6 6.0 %all-to-all-start = ((bf16[1,1,8,2,9,128,128]{6,5,4,3,1,0,2:T(8,128)(2,1)}), bf16[1,1,8,2,9,128,128]{6,5,4,3,1,0,2:T(8,128)(2,1)}, u32[]{:S(2)}, u32[]{:S(2)}) async-start(bf16[1,1,8,2,9,128,128]{6,5,4,3,1,0,2:T(8,128)(2,1)} %bitcast.154), calls=%async_computation | async-start | bytes 9437184 | tf_op jit(solution)/shard_map/all_to_all | solution.py:94
  6.6 0.0 copy-done
  6.7 0.6 copy.135
  7.3 0.3 fusion.57
  7.6 0.5 maximum_bitcast_fusion.4
  8.1 5.1 %fusion.61 = (bf16[4,8,1,1,2,2,2,32]{7,0,6,5,4,1,3,2:T(4,128)(2,1)S(1)}, f32[4,8,1,1,2,2,2,32]{7,0,6,5,4,1,3,2:T(4,128)S(1)}) fusion(bf16[8,1,1,2,2,2,32,1536]{7,6,5,4,3,2,1,0:T(8,128)(2,1)} %param.4, bf16[4,8,1,1,2,2,1,2,1536]{8,0,7,6,5,4,1,3,2:T(4,128)(2,1)S(1)} %maximum_bitcast_fusion.4, bf16[4,8,1,1,2,2,1,2,1536]{8,0,7,6,5,4,1,3,2:T(4,128)(2,1)S(1)} %bitcast.155), kind=kOutput, calls=%fused_computation.101 | convolution fusion | flops 53485568 | bytes 7913472 | tf_op jit(solution)/shard_map/tzxycpki,rtzxycqpi->rtzxycqk/dot_general | solution.py:25
  13.2 0.1 copy.97
  13.3 0.2 reshape.210
  13.5 3.5 %collective-permute-start.1 = (bf16[4,1,1,1,2,128]{5,0,1,4,3,2:T(4,128)(2,1)S(1)}, bf16[4,1,1,1,2,128]{5,0,1,4,3,2:T(4,128)(2,1)S(1)}, u32[]{:S(2)}, u32[]{:S(2)}) collective-permute-start(bf16[4,1,1,1,2,128]{5,0,1,4,3,2:T(4,128)(2,1)S(1)} %get-tuple-element.40), channel_id=1, source_target_pairs={{0,64},{64,128},{128,192},{192,0},{1,65},{65,129},{129,193},{193,1... | collective-permute-start | bytes 6152 | tf_op jit(solution)/shard_map/ppermute | solution.py:14
  17.0 0.0 collective-permute-start
  17.0 0.1 copy.93
  17.1 0.1 reshape.209
  17.2 26.8 %collective-permute-done.1 = bf16[4,1,1,1,2,128]{5,0,1,4,3,2:T(4,128)(2,1)S(1)} collective-permute-done((bf16[4,1,1,1,2,128]{5,0,1,4,3,2:T(4,128)(2,1)S(1)}, bf16[4,1,1,1,2,128]{5,0,1,4,3,2:T(4,128)(2,1)S(1)}, u32[]{:S(2)}, u32[]{:S(2)}) %collective-permute-start.1) | collective-permute-done | bytes 2080 | tf_op jit(solution)/shard_map/ppermute | solution.py:14
  44.0 4.7 %collective-permute-done = bf16[4,1,1,1,2,128]{5,0,1,4,3,2:T(4,128)(2,1)S(1)} collective-permute-done((bf16[4,1,1,1,2,128]{5,0,1,4,3,2:T(4,128)(2,1)S(1)}, bf16[4,1,1,1,2,128]{5,0,1,4,3,2:T(4,128)(2,1)S(1)}, u32[]{:S(2)}, u32[]{:S(2)}) %collective-permute-start) | collective-permute-done | bytes 2080 | tf_op jit(solution)/shard_map/ppermute | solution.py:15
  48.8 5.7 %collective-permute-start.2 = (bf16[4,10,1,1,2,128]{5,0,1,4,3,2:T(4,128)(2,1)S(1)}, bf16[4,10,1,1,2,128]{5,0,1,4,3,2:T(4,128)(2,1)S(1)}, u32[]{:S(2)}, u32[]{:S(2)}) collective-permute-start(bf16[4,10,1,1,2,128]{5,0,1,4,3,2:T(4,128)(2,1)S(1)} %pad_maximum_fusion.2), channel_id=1, source_target_pairs={{8,0},{16,8},{24,16},{32,24},{40,32},{48,40},{56,48},{0,56},{9,1},... | collective-permute-start | bytes 61448 | tf_op jit(solution)/shard_map/ppermute | solution.py:15
  54.5 0.0 collective-permute-start.3
  54.5 0.8 collective-permute-done.2
  55.4 3.3 collective-permute-done.3
  58.7 0.1 pad_maximum_fusion
  58.7 15.4 %collective-permute-start.4 = (bf16[4,10,3,1,2,128]{5,0,1,4,3,2:T(4,128)(2,1)S(1)}, bf16[4,10,3,1,2,128]{5,0,1,4,3,2:T(4,128)(2,1)S(1)}, u32[]{:S(2)}, u32[]{:S(2)}) collective-permute-start(bf16[4,10,3,1,2,128]{5,0,1,4,3,2:T(4,128)(2,1)S(1)} %pad_maximum_fusion), channel_id=1, source_target_pairs={{1,0},{2,1},{3,2},{4,3},{5,4},{6,5},{7,6},{0,7},{9,8},{10,9},{11,1... | collective-permute-start | bytes 184328 | tf_op jit(solution)/shard_map/ppermute | solution.py:15
  74.1 0.0 collective-permute-start.5
  74.1 1.2 collective-permute-done.4
  75.4 3.9 %collective-permute-done.5 = bf16[4,10,3,1,2,128]{5,0,1,4,3,2:T(4,128)(2,1)S(1)} collective-permute-done((bf16[4,10,3,1,2,128]{5,0,1,4,3,2:T(4,128)(2,1)S(1)}, bf16[4,10,3,1,2,128]{5,0,1,4,3,2:T(4,128)(2,1)S(1)}, u32[]{:S(2)}, u32[]{:S(2)}) %collective-permute-start.5) | collective-permute-done | bytes 61472 | tf_op jit(solution)/shard_map/ppermute | solution.py:14
  79.3 0.0 all-to-all-done
  79.3 4.0 %multiply_reduce_fusion.3 = (f32[4]{0:T(128)S(1)}, f32[4]{0:T(128)S(1)}, f32[4,8,1,1,2,128]{5,0,1,4,3,2:T(4,128)S(1)}) fusion(f32[4,8,1,1,2,128]{5,0,1,4,3,2:T(4,128)S(1)} %reshape.210, bf16[1,1,8,2,9,128,128]{6,5,4,3,1,0,2:T(8,128)(2,1)} %all-to-all-done, bf16[4,8,1,1,2,9,128]{6,0,5,4,1,3,2:T(4,128)(2,1)S(1)} %constant_dynamic-update-slice_fusion), kind=kOutput, calls=%fused_computation.55 | convolution fusion | flops 18939896 | bytes 4931616 | tf_op jit(solution)/shard_map/tzxydab,rtzxydb->rtzxya/dot_general | solution.py:63
  83.3 75.2 %all-reduce.1 = (f32[4]{0:T(128)S(1)}, f32[4]{0:T(128)S(1)}) all-reduce(f32[4]{0:T(128)S(1)} %get-tuple-element.11, f32[4]{0:T(128)S(1)} %get-tuple-element.10), channel_id=1, replica_groups=mesh['ta'=4,'gz'=8,'xy'=8] {'ta','gz','xy'}, use_global_device_ids=true, to_apply=%region_1.2 | all-reduce | flops 8 | bytes 64 | tf_op jit(solution)/shard_map/psum | solution.py:96
  158.5 0.1 constant_dynamic-update-slice_fusion.17
  158.6 1.1 collective-permute-start.6
  159.7 2.2 collective-permute-start.7
  162.0 1.3 collective-permute-done.6
  163.2 0.0 collective-permute-done.7
  163.2 1.0 collective-permute-start.8
  164.2 0.7 collective-permute-start.9
  165.0 1.1 collective-permute-done.8
  166.1 1.9 collective-permute-done.9
  168.1 0.1 pad_maximum_fusion.1
  168.1 1.3 collective-permute-start.10
  169.4 0.3 collective-permute-start.11
  169.7 1.6 collective-permute-done.10
  171.3 3.3 collective-permute-done.11
  174.7 3.9 %multiply_reduce_fusion.2 = (f32[4]{0:T(128)S(1)}, f32[4,8,1,1,2,128]{5,0,1,4,3,2:T(4,128)S(1)}) fusion(f32[4,8,1,1,2,128]{5,0,1,4,3,2:T(4,128)S(1)} %get-tuple-element.44, bf16[4,8,1,1,2,128]{5,0,1,4,3,2:T(4,128)(2,1)S(1)} %get-tuple-element.20, bf16[1,1,8,2,9,128,128]{6,5,4,3,1,0,2:T(8,128)(2,1)} %all-to-all-done, ...), kind=kOutput, calls=%fused_computation.53 | convolution fusion | flops 18915324 | bytes 4947984 | tf_op jit(solution)/shard_map/tzxydab,rtzxydb->rtzxya/dot_general | solution.py:63
  178.6 74.8 %psum.37 = f32[4]{0:T(128)S(1)} all-reduce(f32[4]{0:T(128)S(1)} %get-tuple-element.45), channel_id=1, replica_groups=mesh['ta'=4,'gz'=8,'xy'=8] {'ta','gz','xy'}, use_global_device_ids=true, to_apply=%region_5.6 | all-reduce | flops 4 | bytes 32 | tf_op jit(solution)/shard_map/psum | solution.py:103
  253.4 0.2 multiply_reduce_fusion
  253.7 74.5 %all-reduce = (f32[4]{0:T(128)S(1)}, f32[4]{0:T(128)S(1)}) all-reduce(f32[4]{0:T(128)S(1)} %get-tuple-element.9, f32[4]{0:T(128)S(1)} %get-tuple-element.8), channel_id=1, replica_groups=mesh['ta'=4,'gz'=8,'xy'=8] {'ta','gz','xy'}, use_global_device_ids=true, to_apply=%region_7.8 | all-reduce | flops 8 | bytes 64 | tf_op jit(solution)/shard_map/psum | solution.py:107
  328.1 0.1 multiply_subtract_fusion
  328.2 0.1 reshape.202
  328.3 0.1 fusion.58
  328.5 0.1 maximum_bitcast_fusion.7
  328.6 3.9 %fusion.14 = bf16[4,8,1,1,2,2,2,1536]{7,0,6,5,4,1,3,2:T(4,128)(2,1)S(1)} fusion(bf16[8,1,1,2,2,2,32,1536]{7,6,5,4,3,2,1,0:T(8,128)(2,1)} %param.4, bf16[4,8,1,1,2,2,1,2,32]{8,0,7,6,5,4,1,3,2:T(4,128)(2,1)S(1)} %get-tuple-element.31, bf16[4,8,1,1,2,2,1,2,32]{8,0,7,6,5,4,1,3,2:T(4,128)(2,1)S(1)} %get-tuple-element.30), kind=kOutput, calls=%fused_computation.10 | convolution fusion | flops 50790400 | bytes 7110656 | tf_op jit(solution)/shard_map/tzxycpki,rtzxycqpk->rtzxycqi/dot_general | solution.py:38
  332.5 1.5 copy.83
  334.0 0.6 copy.84
  (30 shorter events, 0.5 us)
Async XLA Ops:
  0.6 6.0 %copy-start = (bf16[4,8,1,1,2,2,2,1536]{7,6,5,4,3,2,1,0:T(2,128)(2,1)S(1)}, bf16[4,8,1,1,2,2,2,1536]{7,6,5,4,3,2,1,0:T(2,128)(2,1)}, u32[]{:S(2)}) copy-start(bf16[4,8,1,1,2,2,2,1536]{7,6,5,4,3,2,1,0:T(2,128)(2,1)} %param.3) | copy-start | bytes 2359300
  0.6 78.7 %all-to-all-start = ((bf16[1,1,8,2,9,128,128]{6,5,4,3,1,0,2:T(8,128)(2,1)}), bf16[1,1,8,2,9,128,128]{6,5,4,3,1,0,2:T(8,128)(2,1)}, u32[]{:S(2)}, u32[]{:S(2)}) async-start(bf16[1,1,8,2,9,128,128]{6,5,4,3,1,0,2:T(8,128)(2,1)} %bitcast.154), calls=%async_computation | async-start | bytes 9437184 | tf_op jit(solution)/shard_map/all_to_all | solution.py:94
  13.5 30.6 %collective-permute-start.1 = (bf16[4,1,1,1,2,128]{5,0,1,4,3,2:T(4,128)(2,1)S(1)}, bf16[4,1,1,1,2,128]{5,0,1,4,3,2:T(4,128)(2,1)S(1)}, u32[]{:S(2)}, u32[]{:S(2)}) collective-permute-start(bf16[4,1,1,1,2,128]{5,0,1,4,3,2:T(4,128)(2,1)S(1)} %get-tuple-element.40), channel_id=1, source_target_pairs={{0,64},{64,128},{128,192},{192,0},{1,65},{65,129},{129,193},{193,1... | collective-permute-start | bytes 6152 | tf_op jit(solution)/shard_map/ppermute | solution.py:14
  17.0 31.8 %collective-permute-start = (bf16[4,1,1,1,2,128]{5,0,1,4,3,2:T(4,128)(2,1)S(1)}, bf16[4,1,1,1,2,128]{5,0,1,4,3,2:T(4,128)(2,1)S(1)}, u32[]{:S(2)}, u32[]{:S(2)}) collective-permute-start(bf16[4,1,1,1,2,128]{5,0,1,4,3,2:T(4,128)(2,1)S(1)} %get-tuple-element.41), channel_id=1, source_target_pairs={{64,0},{128,64},{192,128},{0,192},{65,1},{129,65},{193,129},{1,193... | collective-permute-start | bytes 6152 | tf_op jit(solution)/shard_map/ppermute | solution.py:15
  48.8 6.6 %collective-permute-start.2 = (bf16[4,10,1,1,2,128]{5,0,1,4,3,2:T(4,128)(2,1)S(1)}, bf16[4,10,1,1,2,128]{5,0,1,4,3,2:T(4,128)(2,1)S(1)}, u32[]{:S(2)}, u32[]{:S(2)}) collective-permute-start(bf16[4,10,1,1,2,128]{5,0,1,4,3,2:T(4,128)(2,1)S(1)} %pad_maximum_fusion.2), channel_id=1, source_target_pairs={{8,0},{16,8},{24,16},{32,24},{40,32},{48,40},{56,48},{0,56},{9,1},... | collective-permute-start | bytes 61448 | tf_op jit(solution)/shard_map/ppermute | solution.py:15
  54.5 4.2 %collective-permute-start.3 = (bf16[4,10,1,1,2,128]{5,0,1,4,3,2:T(4,128)(2,1)S(1)}, bf16[4,10,1,1,2,128]{5,0,1,4,3,2:T(4,128)(2,1)S(1)}, u32[]{:S(2)}, u32[]{:S(2)}) collective-permute-start(bf16[4,10,1,1,2,128]{5,0,1,4,3,2:T(4,128)(2,1)S(1)} %pad_maximum_fusion.2), channel_id=1, source_target_pairs={{0,8},{8,16},{16,24},{24,32},{32,40},{40,48},{48,56},{56,0},{1,9},... | collective-permute-start | bytes 61448 | tf_op jit(solution)/shard_map/ppermute | solution.py:14
  58.7 16.7 %collective-permute-start.4 = (bf16[4,10,3,1,2,128]{5,0,1,4,3,2:T(4,128)(2,1)S(1)}, bf16[4,10,3,1,2,128]{5,0,1,4,3,2:T(4,128)(2,1)S(1)}, u32[]{:S(2)}, u32[]{:S(2)}) collective-permute-start(bf16[4,10,3,1,2,128]{5,0,1,4,3,2:T(4,128)(2,1)S(1)} %pad_maximum_fusion), channel_id=1, source_target_pairs={{1,0},{2,1},{3,2},{4,3},{5,4},{6,5},{7,6},{0,7},{9,8},{10,9},{11,1... | collective-permute-start | bytes 184328 | tf_op jit(solution)/shard_map/ppermute | solution.py:15
  74.1 5.2 %collective-permute-start.5 = (bf16[4,10,3,1,2,128]{5,0,1,4,3,2:T(4,128)(2,1)S(1)}, bf16[4,10,3,1,2,128]{5,0,1,4,3,2:T(4,128)(2,1)S(1)}, u32[]{:S(2)}, u32[]{:S(2)}) collective-permute-start(bf16[4,10,3,1,2,128]{5,0,1,4,3,2:T(4,128)(2,1)S(1)} %pad_maximum_fusion), channel_id=1, source_target_pairs={{0,1},{1,2},{2,3},{3,4},{4,5},{5,6},{6,7},{7,0},{8,9},{9,10},{10,1... | collective-permute-start | bytes 184328 | tf_op jit(solution)/shard_map/ppermute | solution.py:14
  158.6 4.6 %collective-permute-start.6 = (bf16[4,1,1,1,2,128]{5,0,1,4,3,2:T(4,128)(2,1)S(1)}, bf16[4,1,1,1,2,128]{5,0,1,4,3,2:T(4,128)(2,1)S(1)}, u32[]{:S(2)}, u32[]{:S(2)}) collective-permute-start(bf16[4,1,1,1,2,128]{5,0,1,4,3,2:T(4,128)(2,1)S(1)} %get-tuple-element.35), channel_id=1, source_target_pairs={{64,0},{128,64},{192,128},{0,192},{65,1},{129,65},{193,129},{1,193... | collective-permute-start | bytes 6152 | tf_op jit(solution)/shard_map/ppermute | solution.py:15
  159.7 3.5 %collective-permute-start.7 = (bf16[4,1,1,1,2,128]{5,0,1,4,3,2:T(4,128)(2,1)S(1)}, bf16[4,1,1,1,2,128]{5,0,1,4,3,2:T(4,128)(2,1)S(1)}, u32[]{:S(2)}, u32[]{:S(2)}) collective-permute-start(bf16[4,1,1,1,2,128]{5,0,1,4,3,2:T(4,128)(2,1)S(1)} %get-tuple-element.34), channel_id=1, source_target_pairs={{0,64},{64,128},{128,192},{192,0},{1,65},{65,129},{129,193},{193,1... | collective-permute-start | bytes 6152 | tf_op jit(solution)/shard_map/ppermute | solution.py:14
  163.2 2.9 collective-permute-start.8
  164.2 3.8 %collective-permute-start.9 = (bf16[4,10,1,1,2,128]{5,0,1,4,3,2:T(4,128)(2,1)S(1)}, bf16[4,10,1,1,2,128]{5,0,1,4,3,2:T(4,128)(2,1)S(1)}, u32[]{:S(2)}, u32[]{:S(2)}) collective-permute-start(bf16[4,10,1,1,2,128]{5,0,1,4,3,2:T(4,128)(2,1)S(1)} %pad_maximum_fusion.3), channel_id=1, source_target_pairs={{0,8},{8,16},{16,24},{24,32},{32,40},{40,48},{48,56},{56,0},{1,9},... | collective-permute-start | bytes 61448 | tf_op jit(solution)/shard_map/ppermute | solution.py:14
  168.1 3.1 collective-permute-start.10
  169.4 5.2 %collective-permute-start.11 = (bf16[4,10,3,1,2,128]{5,0,1,4,3,2:T(4,128)(2,1)S(1)}, bf16[4,10,3,1,2,128]{5,0,1,4,3,2:T(4,128)(2,1)S(1)}, u32[]{:S(2)}, u32[]{:S(2)}) collective-permute-start(bf16[4,10,3,1,2,128]{5,0,1,4,3,2:T(4,128)(2,1)S(1)} %pad_maximum_fusion.1), channel_id=1, source_target_pairs={{0,1},{1,2},{2,3},{3,4},{4,5},{5,6},{6,7},{7,0},{8,9},{9,10},{10,1... | collective-permute-start | bytes 184328 | tf_op jit(solution)/shard_map/ppermute | solution.py:14
where the time goes:
time: 335 us
  blocking collectives  224 us (67%)
  waiting for transfers between devices  50 us (15%)
  starting transfers between devices  37.2 us (11%)
  matrix products  16.9 us (5%)
  local copies, waits for them, and re-layouts  3.4 us (1%)
    psum x1, blocking collectives, body(): lax.psum((dotted(image_zero, image_zero), dotted(image_zero, coarse_rhs))...  75.2 us
    psum x1, blocking collectives, body(): coupling = lax.psum(dotted(image_zero, image_one), ('ta', 'gz', 'xy'))  74.8 us
    psum x1, blocking collectives, body(): lax.psum((dotted(image_one, image_one), dotted(image_one, resid_one)), ('...  74.5 us
    ppermute x6, waiting for transfers between devices, padded_2(): before = lax.ppermute(last, axis, up)  39.3 us
    ppermute x6, starting transfers between devices, padded_2(): after = lax.ppermute(initial, axis, down)  24.4 us
    ppermute x6, waiting for transfers between devices, padded_2(): after = lax.ppermute(initial, axis, down)  10.8 us
    dot_general x2, matrix products, combine(): jnp.einsum('tzxydab,rtzxydb->rtzxya', coarse_links, stacked, preferred_el...  7.88 us
    ppermute x6, starting transfers between devices, padded_2(): before = lax.ppermute(last, axis, up)  6.78 us
  transfers between devices with their start and end apart: 13, of which 11 were waited for; matrix products, arithmetic and copies ran while one was open for 2% of the time, Pallas kernels for 0%

commit v1 on v0

v1 whole, which is shorter than its diff:
```python
import jax
import jax.numpy as jnp
from jax import lax
from jax.experimental import pallas as pl
from jax.experimental.pallas import tpu as pltpu
from jax.sharding import PartitionSpec as P

F32 = jnp.float32
BF16 = jnp.bfloat16
RHS = 4
ROWS = 8
DOF = 128
VMEM = pl.BlockSpec(memory_space=pltpu.VMEM)


def call(kernel, out_shape, arguments, flops, bytes_accessed):
    return pl.pallas_call(
        kernel,
        out_shape=out_shape,
        in_specs=[VMEM] * len(arguments),
        out_specs=jax.tree.map(lambda _: VMEM, out_shape),
        compiler_params=pltpu.CompilerParams(vmem_limit_bytes=40 * 1024 * 1024),
        cost_estimate=pl.CostEstimate(flops=flops, bytes_accessed=bytes_accessed, transcendentals=0),
    )(*arguments)


def shape(*dims, dtype=F32):
    return jax.ShapeDtypeStruct(dims, dtype)


def index(dims, dim):
    return lax.broadcasted_iota(jnp.int32, dims, dim)


def dot_nt(left, right):
    return lax.dot_general(left, right, (((1,), (1,)), ((), ())), preferred_element_type=F32)


def dot_nn(left, right):
    return lax.dot_general(left, right, (((1,), (0,)), ((), ())), preferred_element_type=F32)


def swap_halves(field):
    return jnp.concatenate([field[4:], field[:4]], axis=0)


def restrict_kernel(source_ref, vectors_ref, out_ref):
    tile = (ROWS, DOF)
    along = index(tile, 0) < RHS
    chirality = index(tile, 1) < 64
    real = (index(tile, 1) // 32) % 2 == 0
    for time in range(source_ref.shape[0]):
        full = dot_nt(source_ref[time], vectors_ref[time])

        def diagonal(part):
            blocks = []
            for c in range(2):
                row = (part * 2 + c) * ROWS
                rows = full[row : row + ROWS]
                blocks.append(jnp.where(along, rows[:, :DOF], rows[:, DOF:]))
            return jnp.where(chirality, blocks[0], blocks[1])

        first, second = diagonal(0), diagonal(1)
        out_ref[time] = jnp.where(
            real, first + pltpu.roll(second, 96, 1), pltpu.roll(second, 32, 1) - first
        )


def split_rows(field):
    high = field.astype(BF16)
    low = (field - high.astype(F32)).astype(BF16)
    return jnp.concatenate([high, low], axis=0)


def blocks_of(links_ref, across, directions):
    return jnp.concatenate(
        [
            jnp.concatenate([links_ref[across, along, d] for d in directions], axis=1)
            for along in range(2)
        ],
        axis=0,
    )


def hop(links_ref, across, fields, directions):
    total = None
    for start in range(0, len(directions), 2):
        rows = jnp.concatenate([split_rows(f) for f in fields[start : start + 2]], axis=1)
        term = dot_nt(rows, blocks_of(links_ref, across, directions[start : start + 2]))
        total = term if total is None else total + term
    along = (index((2 * ROWS, DOF), 0) // RHS) % 2 == 0
    return jnp.where(along, total[:, :DOF], total[:, DOF:])


def center_kernel(field_ref, links_ref, out_ref):
    sites = field_ref.shape[0]
    for across in range(sites):
        own = field_ref[across]
        swapped = -swap_halves(own)
        fields = [
            own,
            -field_ref[(across + 1) % sites],
            -field_ref[(across - 1) % sites],
            swapped,
            swapped,
        ]
        out_ref[across] = hop(links_ref, across, fields, (0, 5, 6, 7, 8))


def image_kernel(center_ref, field_ref, pt_ref, mt_ref, pz_ref, mz_ref, links_ref, image_ref, full_ref):
    for across in range(field_ref.shape[0]):
        fields = [-ref[across] for ref in (pt_ref, mt_ref, pz_ref, mz_ref)]
        hops = center_ref[across] + hop(links_ref, across, fields, (1, 2, 3, 4))
        own = field_ref[across]
        image = 4.0 * own.astype(BF16).astype(F32) + hops[:ROWS]
        image_ref[across] = image
        full_ref[across] = 4.0 * own + hops[:ROWS] + hops[ROWS:]


PAIRS = ((0, 0), (0, 3), (0, 1), (0, 2), (1, 1), (1, 2), (2, 2), (3, 1), (3, 2))


def second_kernel(
    center_ref, image_ref, pt_ref, mt_ref, pz_ref, mz_ref, links_ref, rhs_ref, full_ref, second_ref, sums_ref
):
    totals = [jnp.zeros((ROWS, DOF), F32) for _ in PAIRS]
    for across in range(image_ref.shape[0]):
        fields = [-ref[across] for ref in (pt_ref, mt_ref, pz_ref, mz_ref)]
        hops = center_ref[across] + hop(links_ref, across, fields, (1, 2, 3, 4))
        image = image_ref[across]
        second = 4.0 * image + hops[:ROWS] + hops[ROWS:]
        second_ref[across] = second
        four = (image, full_ref[across], second, rhs_ref[across])
        for number, (left, right) in enumerate(PAIRS):
            totals[number] = totals[number] + four[left] * four[right]
    lane, row = index((ROWS, DOF), 1), index((ROWS, DOF), 0)
    packed = jnp.zeros((ROWS, DOF), F32)
    for number, total in enumerate(totals):
        one = jnp.sum(total, axis=1, keepdims=True)
        packed = packed + jnp.where(lane == number * RHS + row % RHS, one, 0.0)
    packed = jnp.sum(packed, axis=0, keepdims=True)
    sums_ref[...] = jnp.broadcast_to(packed[None], sums_ref.shape)


def pack_kernel(sums_ref, image_ref, full_ref, second_ref, out_ref):
    partial = jnp.sum(sums_ref[...], axis=0)
    partial = jnp.broadcast_to(partial, (ROWS, DOF))
    for across in range(image_ref.shape[0]):
        out_ref[across, 0:8] = image_ref[across]
        out_ref[across, 8:16] = full_ref[across]
        out_ref[across, 16:24] = second_ref[across]
        out_ref[across, 24:32] = partial


def prolong_kernel(packed_ref, rhs_ref, vectors_ref, correction_ref, residual_ref):
    times = packed_ref.shape[0]
    tile = (ROWS, DOF)
    lane, row = index(tile, 1), index(tile, 0)
    total = packed_ref[0, 24:32]
    for time in range(1, times):
        total = total + packed_ref[time, 24:32]
    gram = [
        jnp.sum(jnp.where(lane == number * RHS + row % RHS, total, 0.0), axis=1, keepdims=True)
        for number in range(len(PAIRS))
    ]
    qq, qr, qs, qw, ss, sw, ww, rs, rw = gram
    alpha_zero = qr / qq
    beta = (qs - alpha_zero * qw) / qq
    norm = ss - 2.0 * alpha_zero * sw + alpha_zero * alpha_zero * ww - beta * beta * qq
    alpha_one = (rs - alpha_zero * rw - beta * qr) / norm
    keep_rhs = alpha_zero + alpha_one * (1.0 - beta)
    keep_image = -alpha_one * alpha_zero
    take_image = alpha_zero - alpha_one * beta

    along = row < RHS
    chirality = lane < 64
    real = (lane // 32) % 2 == 0
    spread = (index((32, 32), 1) == (
        (index((32, 32), 0) % 2) * 16
        + ((index((32, 32), 0) // 8) % 2) * 8
        + (index((32, 32), 0) // 16) * 4
        + (index((32, 32), 0) // 2) % 4
    ))
    spread = jnp.where(spread, 1.0, 0.0).astype(BF16)
    for time in range(times):
        rhs = rhs_ref[time]
        image, full, second = (packed_ref[time, i : i + 8] for i in (0, 8, 16))
        residual = rhs - take_image * image - alpha_one * full + (alpha_one * alpha_zero) * second
        for r in range(RHS):
            for y in range(2):
                residual_ref[r, time, 0, 0, y : y + 1] = residual[y * RHS + r : y * RHS + r + 1]
        value = keep_rhs * rhs + keep_image * image
        value = value.astype(BF16).astype(F32)
        firsts = jnp.where(real, value, -value)
        seconds = jnp.where(real, pltpu.roll(value, 96, 1), pltpu.roll(value, 32, 1))
        rows = []
        for part in (firsts, seconds):
            for c in range(2):
                own = jnp.where(chirality == (c == 0), part, 0.0)
                rows.append(jnp.concatenate([jnp.where(along, own, 0.0), jnp.where(along, 0.0, own)], axis=1))
        left = jnp.concatenate(rows, axis=0).astype(BF16)
        left = dot_nn(spread, left).astype(BF16)
        fields = dot_nn(left, vectors_ref[time]).astype(BF16)
        for y in range(2):
            for c in range(2):
                for r in range(RHS):
                    at = ((y * 2 + c) * RHS + r) * 2
                    correction_ref[r, time, 0, 0, y, c] = fields[at : at + 2]


def shifted(array, axis, step):
    devices = lax.axis_size(axis)
    return lax.ppermute(array, axis, [((i + step) % devices, i) for i in range(devices)])


def neighbours(field):
    across_time = ("ta", "xy")
    return (
        shifted(field, across_time, 1),
        shifted(field, across_time, -1),
        shifted(field, "gz", 1),
        shifted(field, "gz", -1),
    )


def exchange(array, axis):
    return lax.all_to_all(array, axis, split_axis=0, concat_axis=0, tiled=True)


def body(fine_source, vectors, coarse_links):
    times = vectors.shape[0]
    sites = coarse_links.shape[2]
    source = fine_source.reshape(RHS, times, 2, 2, 2, -1).transpose(1, 4, 3, 2, 0, 5)
    source = source.reshape(times, 32, -1)
    vectors = vectors.reshape(times, 256, -1)
    links = coarse_links.reshape(coarse_links.shape[2:])
    field = (sites, ROWS, DOF)
    doubled = (sites, 2 * ROWS, DOF)

    fine_rhs = call(
        restrict_kernel, shape(times, ROWS, DOF), (source, vectors), 2 * times * 32 * 256 * 1536, 7_000_000
    )
    rhs = exchange(fine_rhs, "xy")
    around = neighbours(rhs)
    center = call(center_kernel, shape(*doubled), (rhs, links), 2 * sites * 5 * 16 * 256 * 128, 3_000_000)
    image, full = call(
        image_kernel,
        (shape(*field), shape(*field)),
        (center, rhs, *around, links),
        2 * sites * 4 * 16 * 256 * 128,
        2_000_000,
    )
    around = neighbours(image)
    center = call(center_kernel, shape(*doubled), (image, links), 2 * sites * 5 * 16 * 256 * 128, 3_000_000)
    second, sums = call(
        second_kernel,
        (shape(*field), shape(lax.axis_size("ta") * lax.axis_size("gz"), 1, DOF)),
        (center, image, *around, links, rhs, full),
        2 * sites * 4 * 16 * 256 * 128,
        2_000_000,
    )
    sums = exchange(sums, ("ta", "gz"))
    packed = call(pack_kernel, shape(sites, 32, DOF), (sums, image, full, second), 100_000, 200_000)
    packed = exchange(packed, "xy")
    correction, residual = call(
        prolong_kernel,
        (
            shape(RHS, times, 1, 1, 2, 2, 2, vectors.shape[2], dtype=BF16),
            shape(RHS, times, 1, 1, 2, DOF),
        ),
        (packed, fine_rhs, vectors),
        2 * times * 32 * 256 * 1536,
        7_000_000,
    )
    return (correction, residual)


def solution(mesh):
    return jax.shard_map(
        body,
        mesh=mesh,
        in_specs=(
            P(None, "ta", "gz", "xy", None, None, None, None),
            P("ta", "gz", "xy", None, None, None, None, None),
            P(("ta", "xy"), "gz", None, None, None, None, None),
        ),
        out_specs=(
            P(None, "ta", "gz", "xy", None, None, None, None),
            P(None, "ta", "gz", "xy", None, None),
        ),
        check_vma=False,
    )
```

time: 335 us -> 74 us (0.22)
  blocking collectives: 224 us -> 42.1 us
  waiting for transfers between devices: 50 us -> 1.62 us
  starting transfers between devices: 37.2 us -> 16.5 us
  matrix products: 16.9 us -> 0 us
  Pallas kernels: 0 us -> 7.88 us
    psum x3 -> x0, blocking collectives: 224 us -> none  [the longest x1 75.2 us: body(): lax.psum((dotted(image_zero, image_zero), dotted(image_zero, coarse_rhs))...]
    ppermute x12 -> x8, waiting for transfers between devices: 50 us -> 1.62 us  [shifted(): lax.ppermute(array, axis, [((i + step) % devices, i) for i in range(devic...]
    all_to_all x0 -> x3, blocking collectives: none -> 42.1 us  [exchange(): return lax.all_to_all(array, axis, split_axis=0, concat_axis=0, tiled=True)]
    dot_general x4 -> x0, matrix products: 16.9 us -> none  [the longest x2 7.88 us: combine(): jnp.einsum('tzxydab,rtzxydb->rtzxya', coarse_links, stacked, preferred_el...]
    ppermute x12 -> x8, starting transfers between devices: 31.2 us -> 16.5 us  [shifted(): lax.ppermute(array, axis, [((i + step) % devices, i) for i in range(devic...]
    pallas_call x0 -> x7, Pallas kernels: none -> 7.88 us  [call(): pl.pallas_call(kernel, out_shape=out_shape, in_specs=[VMEM] * len(argumen...]
    all_to_all x1 -> x0, starting transfers between devices: 6.01 us -> none  [body(): lax.all_to_all(coarse_links, 'xy', split_axis=2, concat_axis=0, tiled=True)]
  transfers between devices with their start and end apart: 13 -> 8, of which waited for: 11 -> 2; matrix products, arithmetic and copies ran while one was open for 2% -> 0% of each run, Pallas kernels for 0% -> 2%
where the time goes in v1:
time: 74 us; the launch traced here: 73.7 us
  blocking collectives  42.1 us (57%)
  starting transfers between devices  16.5 us (22%)
  Pallas kernels  7.88 us (11%)
  local copies, waits for them, and re-layouts  4.87 us (7%)
  waiting for transfers between devices  1.62 us (2%)
    all_to_all x3, blocking collectives, exchange(): return lax.all_to_all(array, axis, split_axis=0, concat_axis=0, tiled=True)  42.1 us
    ppermute x8, starting transfers between devices, shifted(): lax.ppermute(array, axis, [((i + step) % devices, i) for i in range(devic...  16.5 us
    pallas_call x7, Pallas kernels, call(): pl.pallas_call(kernel, out_shape=out_shape, in_specs=[VMEM] * len(argumen...  7.88 us
    unnamed x8, local copies, waits for them, and re-layouts  2.94 us
    transpose x1, local copies, waits for them, and re-layouts, body(): fine_source.reshape(RHS, times, 2, 2, 2, -1).transpose(1, 4, 3, 2, 0, 5)  1.74 us
    ppermute x8, waiting for transfers between devices, shifted(): lax.ppermute(array, axis, [((i + step) % devices, i) for i in range(devic...  1.62 us
  transfers between devices with their start and end apart: 8, of which 2 were waited for; matrix products, arithmetic and copies ran while one was open for 0% of the time, Pallas kernels for 2%

profile of v1, /device:TPU:1, one launch (start us, length us, event | category | flops | bytes accessed | tf_op | source)
XLA Modules:
  0.0 73.7 jit_solution(15969786896321162514)
XLA Ops:
  0.6 1.7 %copy.5 = bf16[8,2,2,2,4,1536]{5,4,3,2,1,0:T(4,128)(2,1)S(1)} copy(bf16[8,2,2,2,4,1536]{5,1,2,3,0,4:T(2,128)(2,1)} %bitcast.13) | data formatting | bytes 1572864 | tf_op jit(solution)/shard_map/transpose | solution.py:233
  2.4 0.2 reshape.17.source_ref
  2.6 0.0 copy-start
  2.6 0.0 copy-start.1
  2.6 2.9 %copy-done.1 = bf16[8,1,1,2,2,2,32,1536]{7,6,5,4,3,2,1,0:T(8,128)(2,1)S(1)} copy-done((bf16[8,1,1,2,2,2,32,1536]{7,6,5,4,3,2,1,0:T(8,128)(2,1)S(1)}, bf16[8,1,1,2,2,2,32,1536]{7,6,5,4,3,2,1,0:T(8,128)(2,1)}, u32[]{:S(2)}) %copy-start.1) | copy-done | bytes 6291480
  5.5 2.0 %shard_map.50.rhs_ref = f32[8,8,128]{2,1,0:T(8,128)S(1)} custom-call(bf16[8,32,1536]{2,1,0:T(8,128)(2,1)S(1)} %reshape.17.source_ref, bf16[8,256,1536]{2,1,0:T(8,128)(2,1)S(1)} %bitcast.9), custom_call_target="tpu_custom_call" | custom-call | flops 201326592 | bytes 7000000 | tf_op jit(solution)/shard_map/pallas_call | solution.py:17
  7.5 10.8 %all_to_all.15.field_ref.rhs_ref = f32[8,8,128]{2,1,0:T(8,128)S(1)} all-to-all(f32[8,8,128]{2,1,0:T(8,128)S(1)} %shard_map.50.rhs_ref), channel_id=1, replica_groups=mesh['ta'=4,'gz'=8,'xy'=8] {'xy'}, dimensions={0} | all-to-all | bytes 65536 | tf_op jit(solution)/shard_map/all_to_all | solution.py:227
  18.3 1.6 %collective-permute-start.3 = (f32[8,8,128]{2,1,0:T(8,128)S(1)}, f32[8,8,128]{2,1,0:T(8,128)S(1)}, u32[]{:S(2)}, u32[]{:S(2)}) collective-permute-start(f32[8,8,128]{2,1,0:T(8,128)S(1)} %all_to_all.15.field_ref.rhs_ref), channel_id=1, source_target_pairs={{56,0},{0,8},{8,16},{16,24},{24,32},{32,40},{40,48},{48,56},{57,1}... | collective-permute-start | bytes 98312 | tf_op jit(solution)/shard_map/ppermute | solution.py:213
  19.9 3.9 %collective-permute-start.2 = (f32[8,8,128]{2,1,0:T(8,128)S(1)}, f32[8,8,128]{2,1,0:T(8,128)S(1)}, u32[]{:S(2)}, u32[]{:S(2)}) collective-permute-start(f32[8,8,128]{2,1,0:T(8,128)S(1)} %all_to_all.15.field_ref.rhs_ref), channel_id=1, source_target_pairs={{8,0},{16,8},{24,16},{32,24},{40,32},{48,40},{56,48},{0,56},{9,1},... | collective-permute-start | bytes 98312 | tf_op jit(solution)/shard_map/ppermute | solution.py:213
  23.9 0.4 collective-permute-start.1
  24.2 3.5 %collective-permute-start = (f32[8,8,128]{2,1,0:T(8,128)S(1)}, f32[8,8,128]{2,1,0:T(8,128)S(1)}, u32[]{:S(2)}, u32[]{:S(2)}) collective-permute-start(f32[8,8,128]{2,1,0:T(8,128)S(1)} %all_to_all.15.field_ref.rhs_ref), channel_id=1, source_target_pairs={{1,0},{2,1},{3,2},{4,3},{5,4},{6,5},{7,6},{64,7},{65,64},{66,65},{... | collective-permute-start | bytes 98312 | tf_op jit(solution)/shard_map/ppermute | solution.py:213
  27.7 0.0 copy-done
  27.7 0.8 %shard_map.51.center_ref = f32[8,16,128]{2,1,0:T(8,128)S(1)} custom-call(f32[8,8,128]{2,1,0:T(8,128)S(1)} %all_to_all.15.field_ref.rhs_ref, bf16[8,2,9,128,128]{4,3,2,1,0:T(8,128)(2,1)S(1)} %bitcast.5), custom_call_target="tpu_custom_call" | custom-call | flops 41943040 | bytes 3000000 | tf_op jit(solution)/shard_map/pallas_call | solution.py:17
  28.5 0.0 collective-permute-done.3.mz_ref
  28.5 0.0 collective-permute-done.2.pz_ref
  28.5 0.8 %collective-permute-done.1.mt_ref = f32[8,8,128]{2,1,0:T(8,128)S(1)} collective-permute-done((f32[8,8,128]{2,1,0:T(8,128)S(1)}, f32[8,8,128]{2,1,0:T(8,128)S(1)}, u32[]{:S(2)}, u32[]{:S(2)}) %collective-permute-start.1) | collective-permute-done | bytes 32800 | tf_op jit(solution)/shard_map/ppermute | solution.py:213
  29.3 0.0 collective-permute-done.pt_ref
  29.3 0.0 slice-start
  29.3 0.6 shard_map.52
  30.0 0.0 slice-start.1
  30.0 0.0 collective-permute-start.7
  30.0 2.7 %collective-permute-start.6 = (f32[8,8,128]{2,1,0:T(8,128)S(1)}, f32[8,8,128]{2,1,0:T(8,128)S(1)}, u32[]{:S(2)}, u32[]{:S(2)}) collective-permute-start(f32[8,8,128]{2,1,0:T(8,128)S(1)} %get-tuple-element.6.field_ref.image_ref), channel_id=1, source_target_pairs={{8,0},{16,8},{24,16},{32,24},{40,32},{48,40},{56,48},{0,56},{9,1},... | collective-permute-start | bytes 98312 | tf_op jit(solution)/shard_map/ppermute | solution.py:213
  32.7 0.0 collective-permute-start.5
  32.7 4.4 %collective-permute-start.4 = (f32[8,8,128]{2,1,0:T(8,128)S(1)}, f32[8,8,128]{2,1,0:T(8,128)S(1)}, u32[]{:S(2)}, u32[]{:S(2)}) collective-permute-start(f32[8,8,128]{2,1,0:T(8,128)S(1)} %get-tuple-element.6.field_ref.image_ref), channel_id=1, source_target_pairs={{1,0},{2,1},{3,2},{4,3},{5,4},{6,5},{7,6},{64,7},{65,64},{66,65},{... | collective-permute-start | bytes 98312 | tf_op jit(solution)/shard_map/ppermute | solution.py:213
  37.1 0.8 %shard_map.53.center_ref = f32[8,16,128]{2,1,0:T(8,128)S(1)} custom-call(f32[8,8,128]{2,1,0:T(8,128)S(1)} %get-tuple-element.6.field_ref.image_ref, bf16[8,2,9,128,128]{4,3,2,1,0:T(8,128)(2,1)S(1)} %bitcast.7), custom_call_target="tpu_custom_call" | custom-call | flops 41943040 | bytes 3000000 | tf_op jit(solution)/shard_map/pallas_call | solution.py:17
  37.8 0.0 collective-permute-done.7.mz_ref
  37.8 0.0 collective-permute-done.6.pz_ref
  37.9 0.8 %collective-permute-done.5.mt_ref = f32[8,8,128]{2,1,0:T(8,128)S(1)} collective-permute-done((f32[8,8,128]{2,1,0:T(8,128)S(1)}, f32[8,8,128]{2,1,0:T(8,128)S(1)}, u32[]{:S(2)}, u32[]{:S(2)}) %collective-permute-start.5) | collective-permute-done | bytes 32800 | tf_op jit(solution)/shard_map/ppermute | solution.py:213
  38.7 0.0 collective-permute-done.4.pt_ref
  38.7 0.8 %shard_map.54 = (f32[8,8,128]{2,1,0:T(8,128)S(1)}, f32[32,1,128]{2,1,0:T(1,128)S(1)}) custom-call(f32[8,16,128]{2,1,0:T(8,128)S(1)} %shard_map.53.center_ref, f32[8,8,128]{2,1,0:T(8,128)S(1)} %get-tuple-element.6.field_ref.image_ref, f32[8,8,128]{2,1,0:T(8,128)S(1)} %collective-permute-done.4.pt_ref, f32[8,8,128]{2,1,0:T(8,128)S(1)} %collective-permute-done.5.mt_ref, ...), custom_call_target="tpu_custom_call" | custom-call | flops 33554432 | bytes 2000000 | tf_op jit(solution)/shard_map/pallas_call | solution.py:17
  39.4 19.9 %all_to_all.16.sums_ref = f32[32,1,128]{2,1,0:T(1,128)S(1)} all-to-all(f32[32,1,128]{2,1,0:T(1,128)S(1)} %get-tuple-element.8), channel_id=1, replica_groups=mesh['ta'=4,'gz'=8,'xy'=8] {'ta','gz'}, dimensions={0} | all-to-all | bytes 32768 | tf_op jit(solution)/shard_map/all_to_all | solution.py:227
  59.4 11.4 %all_to_all.17.packed_ref = f32[8,32,128]{2,1,0:T(8,128)S(1)} all-to-all(f32[8,32,128]{2,1,0:T(8,128)S(1)} %shard_map.55), channel_id=1, replica_groups=mesh['ta'=4,'gz'=8,'xy'=8] {'xy'}, dimensions={0} | all-to-all | bytes 262144 | tf_op jit(solution)/shard_map/all_to_all | solution.py:227
  70.8 0.0 slice-done
  70.8 0.0 slice-done.1
  70.8 2.9 %shard_map.56 = (bf16[4,8,1,1,2,2,2,1536]{7,6,5,4,3,2,1,0:T(2,128)(2,1)}, f32[4,8,1,1,2,128]{5,4,3,2,1,0:T(2,128)}) custom-call(f32[8,32,128]{2,1,0:T(8,128)S(1)} %all_to_all.17.packed_ref, f32[8,8,128]{2,1,0:T(8,128)S(1)} %shard_map.50.rhs_ref, bf16[8,256,1536]{2,1,0:T(8,128)(2,1)S(1)} %bitcast.12), custom_call_target="tpu_custom_call" | custom-call | flops 201326592 | bytes 7000000 | tf_op jit(solution)/shard_map/pallas_call | solution.py:17
  (2 shorter events, 0.0 us)
Async XLA Ops:
  2.6 25.2 %copy-start = (bf16[1,1,8,2,9,128,128]{6,5,4,3,2,1,0:T(8,128)(2,1)S(1)}, bf16[1,1,8,2,9,128,128]{6,5,4,3,2,1,0:T(8,128)(2,1)}, u32[]{:S(2)}) copy-start(bf16[1,1,8,2,9,128,128]{6,5,4,3,2,1,0:T(8,128)(2,1)} %param.5) | copy-start | bytes 14155780
  2.6 2.9 %copy-start.1 = (bf16[8,1,1,2,2,2,32,1536]{7,6,5,4,3,2,1,0:T(8,128)(2,1)S(1)}, bf16[8,1,1,2,2,2,32,1536]{7,6,5,4,3,2,1,0:T(8,128)(2,1)}, u32[]{:S(2)}) copy-start(bf16[8,1,1,2,2,2,32,1536]{7,6,5,4,3,2,1,0:T(8,128)(2,1)} %param.4) | copy-start | bytes 18874372
  18.3 10.2 %collective-permute-start.3 = (f32[8,8,128]{2,1,0:T(8,128)S(1)}, f32[8,8,128]{2,1,0:T(8,128)S(1)}, u32[]{:S(2)}, u32[]{:S(2)}) collective-permute-start(f32[8,8,128]{2,1,0:T(8,128)S(1)} %all_to_all.15.field_ref.rhs_ref), channel_id=1, source_target_pairs={{56,0},{0,8},{8,16},{16,24},{24,32},{32,40},{40,48},{48,56},{57,1}... | collective-permute-start | bytes 98312 | tf_op jit(solution)/shard_map/ppermute | solution.py:213
  19.9 8.6 %collective-permute-start.2 = (f32[8,8,128]{2,1,0:T(8,128)S(1)}, f32[8,8,128]{2,1,0:T(8,128)S(1)}, u32[]{:S(2)}, u32[]{:S(2)}) collective-permute-start(f32[8,8,128]{2,1,0:T(8,128)S(1)} %all_to_all.15.field_ref.rhs_ref), channel_id=1, source_target_pairs={{8,0},{16,8},{24,16},{32,24},{40,32},{48,40},{56,48},{0,56},{9,1},... | collective-permute-start | bytes 98312 | tf_op jit(solution)/shard_map/ppermute | solution.py:213
  23.9 5.4 %collective-permute-start.1 = (f32[8,8,128]{2,1,0:T(8,128)S(1)}, f32[8,8,128]{2,1,0:T(8,128)S(1)}, u32[]{:S(2)}, u32[]{:S(2)}) collective-permute-start(f32[8,8,128]{2,1,0:T(8,128)S(1)} %all_to_all.15.field_ref.rhs_ref), channel_id=1, source_target_pairs={{199,0},{0,1},{1,2},{2,3},{3,4},{4,5},{5,6},{6,7},{7,64},{64,65},{... | collective-permute-start | bytes 98312 | tf_op jit(solution)/shard_map/ppermute | solution.py:213
  24.2 5.1 %collective-permute-start = (f32[8,8,128]{2,1,0:T(8,128)S(1)}, f32[8,8,128]{2,1,0:T(8,128)S(1)}, u32[]{:S(2)}, u32[]{:S(2)}) collective-permute-start(f32[8,8,128]{2,1,0:T(8,128)S(1)} %all_to_all.15.field_ref.rhs_ref), channel_id=1, source_target_pairs={{1,0},{2,1},{3,2},{4,3},{5,4},{6,5},{7,6},{64,7},{65,64},{66,65},{... | collective-permute-start | bytes 98312 | tf_op jit(solution)/shard_map/ppermute | solution.py:213
  29.3 41.5 %slice-start = ((s8[6291456]{0:T(1024)(128)(4,1)}), s8[4194304]{0:T(1024)(128)(4,1)S(1)}, s32[]{:S(2)}) async-start(s8[6291456]{0:T(1024)(128)(4,1)} %bitcast.10), calls=%async_computation.3 | async-start | bytes 8388608
  30.0 40.8 %slice-start.1 = ((s8[6291456]{0:T(1024)(128)(4,1)}), s8[2097152]{0:T(1024)(128)(4,1)S(1)}, s32[]{:S(2)}) async-start(s8[6291456]{0:T(1024)(128)(4,1)} %bitcast.10), calls=%async_computation.4 | async-start | bytes 4194304
  30.0 7.9 %collective-permute-start.7 = (f32[8,8,128]{2,1,0:T(8,128)S(1)}, f32[8,8,128]{2,1,0:T(8,128)S(1)}, u32[]{:S(2)}, u32[]{:S(2)}) collective-permute-start(f32[8,8,128]{2,1,0:T(8,128)S(1)} %get-tuple-element.6.field_ref.image_ref), channel_id=1, source_target_pairs={{56,0},{0,8},{8,16},{16,24},{24,32},{32,40},{40,48},{48,56},{57,1}... | collective-permute-start | bytes 98312 | tf_op jit(solution)/shard_map/ppermute | solution.py:213
  30.0 7.9 %collective-permute-start.6 = (f32[8,8,128]{2,1,0:T(8,128)S(1)}, f32[8,8,128]{2,1,0:T(8,128)S(1)}, u32[]{:S(2)}, u32[]{:S(2)}) collective-permute-start(f32[8,8,128]{2,1,0:T(8,128)S(1)} %get-tuple-element.6.field_ref.image_ref), channel_id=1, source_target_pairs={{8,0},{16,8},{24,16},{32,24},{40,32},{48,40},{56,48},{0,56},{9,1},... | collective-permute-start | bytes 98312 | tf_op jit(solution)/shard_map/ppermute | solution.py:213
  32.7 6.0 %collective-permute-start.5 = (f32[8,8,128]{2,1,0:T(8,128)S(1)}, f32[8,8,128]{2,1,0:T(8,128)S(1)}, u32[]{:S(2)}, u32[]{:S(2)}) collective-permute-start(f32[8,8,128]{2,1,0:T(8,128)S(1)} %get-tuple-element.6.field_ref.image_ref), channel_id=1, source_target_pairs={{199,0},{0,1},{1,2},{2,3},{3,4},{4,5},{5,6},{6,7},{7,64},{64,65},{... | collective-permute-start | bytes 98312 | tf_op jit(solution)/shard_map/ppermute | solution.py:213
  32.7 6.0 %collective-permute-start.4 = (f32[8,8,128]{2,1,0:T(8,128)S(1)}, f32[8,8,128]{2,1,0:T(8,128)S(1)}, u32[]{:S(2)}, u32[]{:S(2)}) collective-permute-start(f32[8,8,128]{2,1,0:T(8,128)S(1)} %get-tuple-element.6.field_ref.image_ref), channel_id=1, source_target_pairs={{1,0},{2,1},{3,2},{4,3},{5,4},{6,5},{7,6},{64,7},{65,64},{66,65},{... | collective-permute-start | bytes 98312 | tf_op jit(solution)/shard_map/ppermute | solution.py:213

commit v2 on v1

v2 whole, which is shorter than its diff:
```python
import jax
import jax.numpy as jnp
from jax import lax
from jax.experimental import pallas as pl
from jax.experimental.pallas import tpu as pltpu
from jax.sharding import PartitionSpec as P

F32 = jnp.float32
BF16 = jnp.bfloat16
RHS = 4
LIMIT = 52
ROWS = 8
DOF = 128
VMEM = pl.BlockSpec(memory_space=pltpu.VMEM)


def call(kernel, out_shape, arguments, flops, bytes_accessed, inputs=VMEM, outputs=None, scratch=(), limit=16):
    return pl.pallas_call(
        kernel,
        out_shape=out_shape,
        in_specs=[inputs] * len(arguments),
        out_specs=outputs if outputs is not None else ([VMEM] * len(out_shape) if isinstance(out_shape, tuple) else VMEM),
        scratch_shapes=scratch,
        compiler_params=pltpu.CompilerParams(vmem_limit_bytes=limit * 1024 * 1024),
        cost_estimate=pl.CostEstimate(flops=flops, bytes_accessed=bytes_accessed, transcendentals=0),
    )(*arguments)


def shape(*dims, dtype=F32):
    return pltpu.VMEM(dims, dtype)


def index(dims, dim):
    return lax.broadcasted_iota(jnp.int32, dims, dim)


def dot_nt(left, right):
    return lax.dot_general(left, right, (((1,), (1,)), ((), ())), preferred_element_type=F32)


def dot_nn(left, right):
    return lax.dot_general(left, right, (((1,), (0,)), ((), ())), preferred_element_type=F32)


def swap_halves(field):
    return jnp.concatenate([field[4:], field[:4]], axis=0)


def restrict_kernel(
    source_hbm, vectors_hbm, links_hbm, out_ref, vectors, links, source, rows, full, source_sem, vectors_sem, links_sem
):
    times = vectors.shape[0]
    half = times // 2
    groups = (range(half), range(half, times))
    whole = pltpu.make_async_copy(source_hbm, source, source_sem)
    whole.start()
    copies = []
    for number, group in enumerate(groups):
        span = pl.ds(group[0], len(group))
        copy = pltpu.make_async_copy(vectors_hbm.at[span, 0, 0], vectors.at[span], vectors_sem.at[number])
        copy.start()
        copies.append(copy)
    blocks = pltpu.make_async_copy(links_hbm.at[0, 0], links, links_sem)
    blocks.start()
    tile = (ROWS, DOF)
    along = index(tile, 0) < RHS
    chirality = index(tile, 1) < 64
    real = (index(tile, 1) // 32) % 2 == 0

    def gather(group):
        for time in group:
            for c in range(2):
                for y in range(2):
                    for r in range(RHS):
                        at = ((c * 2 + y) * RHS + r) * 2
                        rows[time, at : at + 2] = source[r, time, 0, 0, y, c]

    def diagonal(time, part):
        one, two = (full[time, y, pl.ds(part, 2 * ROWS, 2), :] for y in range(2))
        picked = [jnp.where(along, one[at : at + ROWS], two[at : at + ROWS]) for at in (0, ROWS)]
        return jnp.where(chirality, picked[0], picked[1])

    def combine(group):
        for time in group:
            first, second = diagonal(time, 0), diagonal(time, 1)
            out_ref[time] = jnp.where(
                real, first + pltpu.roll(second, 96, 1), pltpu.roll(second, 32, 1) - first
            )

    whole.wait()
    gather(groups[0])
    for number, group in enumerate(groups):
        copies[number].wait()
        for time in group:
            product = dot_nt(rows[time], vectors[time].reshape(256, -1))
            full[time, 0], full[time, 1] = product[:, :DOF], product[:, DOF:]
        if number == 0:
            gather(groups[1])
        else:
            combine(groups[0])
    combine(groups[1])
    blocks.wait()


def split_rows(field):
    high = field.astype(BF16)
    low = (field - high.astype(F32)).astype(BF16)
    return jnp.concatenate([high, low], axis=0)


def blocks_of(links_ref, across, directions):
    return jnp.concatenate(
        [
            jnp.concatenate([links_ref[across, along, d] for d in directions], axis=1)
            for along in range(2)
        ],
        axis=0,
    )


def hop(links_ref, across, fields, directions):
    total = None
    for start in range(0, len(directions), 2):
        rows = jnp.concatenate([split_rows(f) for f in fields[start : start + 2]], axis=1)
        term = dot_nt(rows, blocks_of(links_ref, across, directions[start : start + 2]))
        total = term if total is None else total + term
    along = (index((2 * ROWS, DOF), 0) // RHS) % 2 == 0
    return jnp.where(along, total[:, :DOF], total[:, DOF:])


def center_kernel(field_ref, links_ref, out_ref):
    sites = field_ref.shape[0]
    for across in range(sites):
        own = field_ref[across]
        swapped = -swap_halves(own)
        fields = [
            own,
            -field_ref[(across + 1) % sites],
            -field_ref[(across - 1) % sites],
            swapped,
            swapped,
        ]
        out_ref[across] = hop(links_ref, across, fields, (0, 5, 6, 7, 8))


def around_directions():
    time, depth = lax.axis_index("xy") % 2, lax.axis_index("gz") % 2
    return (1 + time, 2 - time, 3 + depth, 4 - depth)


def image_kernel(center_ref, field_ref, t0_ref, t1_ref, z0_ref, z1_ref, links_ref, image_ref, rest_ref):
    directions = around_directions()
    for across in range(field_ref.shape[0]):
        fields = [-ref[across] for ref in (t0_ref, t1_ref, z0_ref, z1_ref)]
        hops = center_ref[across] + hop(links_ref, across, fields, directions)
        own = field_ref[across]
        rounded = own.astype(BF16).astype(F32)
        image_ref[across] = 4.0 * rounded + hops[:ROWS]
        rest_ref[across] = 4.0 * (own - rounded) + hops[ROWS:]


PAIRS = ((0, 0), (0, 1), (2, 2), (2, 3), (3, 3), (0, 2), (0, 3), (2, 1), (3, 1))


def second_kernel(
    center_ref, image_ref, t0_ref, t1_ref, z0_ref, z1_ref, links_ref, rhs_ref, rest_ref, out_ref
):
    directions = around_directions()
    totals = [jnp.zeros((ROWS, DOF), F32) for _ in PAIRS]
    for across in range(image_ref.shape[0]):
        fields = [-ref[across] for ref in (t0_ref, t1_ref, z0_ref, z1_ref)]
        hops = center_ref[across] + hop(links_ref, across, fields, directions)
        hops = hops[:ROWS] + hops[ROWS:]
        image, rest = image_ref[across], rest_ref[across]
        out_ref[across, 0:8] = image
        out_ref[across, 8:16] = rest
        out_ref[across, 16:24] = hops
        four = (image, image - 4.0 * rhs_ref[across], hops, rest)
        for number, (left, right) in enumerate(PAIRS):
            totals[number] = totals[number] + four[left] * four[right]
    lane, row = index((ROWS, DOF), 1), index((ROWS, DOF), 0)
    packed = jnp.zeros((ROWS, DOF), F32)
    for number, total in enumerate(totals):
        one = jnp.sum(total, axis=1, keepdims=True)
        packed = packed + jnp.where(lane == number * RHS + row % RHS, one, 0.0)
    packed = packed + jnp.concatenate([packed[4:], packed[:4]], axis=0)
    for across in range(image_ref.shape[0]):
        out_ref[across, 24:32] = packed


def sums_kernel(packed_ref, out_ref):
    total = packed_ref[0, 24:32]
    for peer in range(1, packed_ref.shape[0]):
        total = total + packed_ref[peer, 24:32]
    total = jnp.where(index((ROWS, DOF), 1) % RHS == index((ROWS, DOF), 0), total, 0.0)
    total = jnp.sum(total, axis=0, keepdims=True)
    out_ref[...] = jnp.broadcast_to(total[None], out_ref.shape)


def block_rows(value):
    tile = (ROWS, DOF)
    along = index(tile, 0) < RHS
    chirality = index(tile, 1) < 64
    real = (index(tile, 1) // 32) % 2 == 0
    firsts = jnp.where(real, value, -value)
    seconds = jnp.where(real, pltpu.roll(value, 96, 1), pltpu.roll(value, 32, 1))
    rows = []
    for part in (firsts, seconds):
        for c in range(2):
            own = jnp.where(chirality == (c == 0), part, 0.0)
            rows.append(jnp.concatenate([jnp.where(along, own, 0.0), jnp.where(along, 0.0, own)], axis=1))
    return jnp.concatenate(rows, axis=0)


def basis_kernel(packed_ref, rhs_ref, vectors_ref, out_ref):
    row, column = index((32, 32), 0), index((32, 32), 1)
    order = column == (row % 2) * 16 + ((row // 8) % 2) * 8 + (row // 16) * 4 + (row // 2) % 4
    order = jnp.where(order, 1.0, 0.0).astype(BF16)
    for time in range(packed_ref.shape[0]):
        parts = []
        for field in (rhs_ref[time], packed_ref[time, 0:8]):
            high = field.astype(BF16).astype(F32)
            for part in (high, field - high):
                parts.append(dot_nn(order, block_rows(part).astype(BF16)).astype(BF16))
        fields = dot_nn(jnp.concatenate(parts, axis=0), vectors_ref[time].reshape(256, -1))
        out_ref[time, 0:32] = fields[0:32] + fields[32:64]
        out_ref[time, 32:64] = fields[64:96] + fields[96:128]


def coefficients(total, numbers):
    lane = index(numbers.shape, 1)
    spread = jnp.broadcast_to(total, numbers.shape)
    gram = [
        jnp.sum(jnp.where(lane == number * RHS + numbers, spread, 0.0), axis=1, keepdims=True)
        for number in range(len(PAIRS))
    ]
    qq, qn, zz, ze, ee, qz, qe, zn, en = gram
    gamma = qn / qq
    alpha_zero = 0.25 * (1.0 - gamma)
    hh = ee - 2.0 * alpha_zero * ze + alpha_zero * alpha_zero * zz
    kappa = (qe - alpha_zero * qz) / qq
    norm = hh - kappa * kappa * qq
    alpha_one = -0.25 * (en - alpha_zero * zn - kappa * qn) / norm
    return alpha_zero, alpha_one, gamma + kappa, kappa


def finish_kernel(sums_ref, packed_ref, rhs_ref, basis_ref, correction_hbm, residual_ref, correction, sems):
    times = packed_ref.shape[0]
    total = jnp.sum(sums_ref[...], axis=0)
    alpha_zero, alpha_one, beta, kappa = coefficients(total, (index((32, DOF), 0) // 2) % RHS)
    keep_rhs = alpha_zero + alpha_one * (1.0 - beta)
    keep_image = -alpha_one * alpha_zero
    copies = []
    for time in range(times):
        fields = (keep_rhs * basis_ref[time, 0:32] + keep_image * basis_ref[time, 32:64]).astype(BF16)
        for y in range(2):
            for c in range(2):
                for r in range(RHS):
                    at = ((y * 2 + c) * RHS + r) * 2
                    correction[r, time, 0, 0, y, c] = fields[at : at + 2]
        copy = pltpu.make_async_copy(correction.at[:, time], correction_hbm.at[:, time], sems.at[time])
        copy.start()
        copies.append(copy)
    alpha_zero, alpha_one, beta, kappa = coefficients(total, index((ROWS, DOF), 0) % RHS)
    for time in range(times):
        image, rest, hops = (packed_ref[time, i : i + 8] for i in (0, 8, 16))
        residual = rhs_ref[time] - (alpha_zero - alpha_one * kappa) * image
        residual = residual - alpha_one * (rest - alpha_zero * hops)
        for r in range(RHS):
            for y in range(2):
                residual_ref[r, time, 0, 0, y : y + 1] = residual[y * RHS + r : y * RHS + r + 1]
    for copy in copies:
        copy.wait()


def neighbours(field):
    found = []
    for axis in (("ta", "xy"), "gz"):
        devices = lax.axis_size(axis)
        for first in range(2):
            pairs = [(i, (i + 1) % devices) for i in range(first, devices, 2)]
            found.append(lax.ppermute(field, axis, pairs + [(j, i) for i, j in pairs]))
    return found


def exchange(array, axis):
    return lax.all_to_all(array, axis, split_axis=0, concat_axis=0, tiled=True)


def body(fine_source, vectors, coarse_links):
    times = vectors.shape[0]
    sites = coarse_links.shape[2]
    field = (sites, ROWS, DOF)
    doubled = (sites, 2 * ROWS, DOF)
    length = vectors.shape[-1]

    anywhere = pl.BlockSpec(memory_space=pl.ANY)
    fine_rhs, vectors, links = call(
        restrict_kernel,
        (
            shape(times, ROWS, DOF),
            shape(*vectors.shape[:1], *vectors.shape[3:], dtype=BF16),
            shape(*coarse_links.shape[2:], dtype=BF16),
        ),
        (fine_source, vectors, coarse_links),
        2 * times * 32 * 256 * length,
        12_000_000,
        inputs=anywhere,
        scratch=[
            pltpu.VMEM(fine_source.shape, BF16),
            pltpu.VMEM((times, 32, length), BF16),
            pltpu.VMEM((times, 2, 32, DOF), F32),
            pltpu.SemaphoreType.DMA,
            pltpu.SemaphoreType.DMA((2,)),
            pltpu.SemaphoreType.DMA,
        ],
        limit=LIMIT,
    )
    rhs = exchange(fine_rhs, "xy")
    around = neighbours(rhs)
    center = call(center_kernel, shape(*doubled), (rhs, links), 2 * sites * 5 * 16 * 256 * 128, 3_000_000)
    image, rest = call(
        image_kernel,
        (shape(*field), shape(*field)),
        (center, rhs, *around, links),
        2 * sites * 4 * 16 * 256 * 128,
        2_000_000,
    )
    around = neighbours(image)
    center = call(center_kernel, shape(*doubled), (image, links), 2 * sites * 5 * 16 * 256 * 128, 3_000_000)
    packed = call(
        second_kernel,
        shape(sites, 32, DOF),
        (center, image, *around, links, rhs, rest),
        2 * sites * 4 * 16 * 256 * 128,
        2_000_000,
    )
    packed = exchange(packed, "xy")
    sums = call(
        sums_kernel, shape(lax.axis_size("ta") * lax.axis_size("gz"), 1, DOF), (packed,), 10_000, 50_000
    )
    sums = exchange(sums, ("ta", "gz"))
    basis = call(
        basis_kernel,
        shape(times, 64, length),
        (packed, fine_rhs, vectors),
        2 * times * 128 * 256 * length,
        10_000_000,
    )
    correction, residual = call(
        finish_kernel,
        (
            jax.ShapeDtypeStruct(fine_source.shape, BF16),
            jax.ShapeDtypeStruct((RHS, times, 1, 1, 2, DOF), F32),
        ),
        (sums, packed, fine_rhs, basis),
        2_000_000,
        4_000_000,
        outputs=(anywhere, VMEM),
        scratch=[pltpu.VMEM(fine_source.shape, BF16), pltpu.SemaphoreType.DMA((times,))],
    )
    return (correction, residual)


def solution(mesh):
    return jax.shard_map(
        body,
        mesh=mesh,
        in_specs=(
            P(None, "ta", "gz", "xy", None, None, None, None),
            P("ta", "gz", "xy", None, None, None, None, None),
            P(("ta", "xy"), "gz", None, None, None, None, None),
        ),
        out_specs=(
            P(None, "ta", "gz", "xy", None, None, None, None),
            P(None, "ta", "gz", "xy", None, None),
        ),
        check_vma=False,
    )
```

time: 74 us -> 66.6 us (0.90)
  blocking collectives: 42.1 us -> 20.3 us
  waiting for transfers between devices: 1.62 us -> 8.93 us
  starting transfers between devices: 16.5 us -> 21.4 us
  Pallas kernels: 7.88 us -> 12.2 us
  local copies, waits for them, and re-layouts: 4.87 us -> 2.78 us
    all_to_all x3 -> x2, blocking collectives: 42.1 us -> 20.3 us  [exchange(): return lax.all_to_all(array, axis, split_axis=0, concat_axis=0, tiled=True)]
    all_to_all x0 -> x1, starting transfers between devices: none -> 7.26 us  [exchange(): return lax.all_to_all(array, axis, split_axis=0, concat_axis=0, tiled=True)]
    pallas_call x7 -> x8, Pallas kernels: 7.88 us -> 12.2 us  [call(): pl.pallas_call(kernel, out_shape=out_shape, in_specs=[inputs] * len(argum...]
    all_to_all x0 -> x1, waiting for transfers between devices: none -> 4.33 us  [exchange(): return lax.all_to_all(array, axis, split_axis=0, concat_axis=0, tiled=True)]
    ppermute x8, waiting for transfers between devices: 1.62 us -> 4.6 us  [neighbours(): found.append(lax.ppermute(field, axis, pairs + [(j, i) for i, j in pairs]))]
    ppermute x8, starting transfers between devices: 16.5 us -> 14.1 us  [neighbours(): found.append(lax.ppermute(field, axis, pairs + [(j, i) for i, j in pairs]))]
    transpose x1 -> x0, local copies, waits for them, and re-layouts: 1.74 us -> none  [body(): fine_source.reshape(RHS, times, 2, 2, 2, -1).transpose(1, 4, 3, 2, 0, 5)]
    unnamed x8 -> x4, local copies, waits for them, and re-layouts: 2.94 us -> 2.78 us
  transfers between devices with their start and end apart: 8 -> 9, of which waited for: 2 -> 5; matrix products, arithmetic and copies ran while one was open for 0% -> 0% of each run, Pallas kernels for 2% -> 6%
where the time goes in v2:
time: 66.6 us; the launch traced here: 66.3 us
  starting transfers between devices  21.4 us (32%)
  blocking collectives  20.3 us (30%)
  Pallas kernels  12.2 us (18%)
  waiting for transfers between devices  8.93 us (13%)
  local copies, waits for them, and re-layouts  2.78 us (4%)
  between operations  0.7 us (1%)
    all_to_all x2, blocking collectives, exchange(): return lax.all_to_all(array, axis, split_axis=0, concat_axis=0, tiled=True)  20.3 us
    ppermute x8, starting transfers between devices, neighbours(): found.append(lax.ppermute(field, axis, pairs + [(j, i) for i, j in pairs]))  14.1 us
    pallas_call x8, Pallas kernels, call(): pl.pallas_call(kernel, out_shape=out_shape, in_specs=[inputs] * len(argum...  12.2 us
    all_to_all x1, starting transfers between devices, exchange(): return lax.all_to_all(array, axis, split_axis=0, concat_axis=0, tiled=True)  7.26 us
    ppermute x8, waiting for transfers between devices, neighbours(): found.append(lax.ppermute(field, axis, pairs + [(j, i) for i, j in pairs]))  4.6 us
    all_to_all x1, waiting for transfers between devices, exchange(): return lax.all_to_all(array, axis, split_axis=0, concat_axis=0, tiled=True)  4.33 us
    unnamed x4, local copies, waits for them, and re-layouts  2.78 us
  transfers between devices with their start and end apart: 9, of which 5 were waited for; matrix products, arithmetic and copies ran while one was open for 0% of the time, Pallas kernels for 6%

profile of v2, /device:TPU:1, one launch (start us, length us, event | category | flops | bytes accessed | tf_op | source)
XLA Modules:
  0.0 66.3 jit_solution(10435216611699574038)
XLA Ops:
  0.6 4.6 %shard_map.50 = (f32[8,8,128]{2,1,0:T(8,128)S(1)}, bf16[8,2,2,2,32,1536]{5,4,3,2,1,0:T(8,128)(2,1)S(1)}, bf16[8,2,9,128,128]{4,3,2,1,0:T(8,128)(2,1)S(1)}) custom-call(bf16[4,8,1,1,2,2,2,1536]{7,6,5,4,3,2,1,0:T(2,128)(2,1)} %source_hbm.1, bf16[8,1,1,2,2,2,32,1536]{7,6,5,4,3,2,1,0:T(8,128)(2,1)} %vectors_hbm.1, bf16[1,1,8,2,9,128,128]{6,5,4,3,2,1,0:T(8,128)(2,1)} %links_hbm.1), custom_call_target="tpu_custom_call" | custom-call | flops 201326592 | bytes 12000000 | tf_op jit(solution)/shard_map/pallas_call | solution.py:18
  5.3 0.0 copy-start
  5.3 10.8 %all_to_all.15.field_ref.rhs_ref = f32[8,8,128]{2,1,0:T(8,128)S(1)} all-to-all(f32[8,8,128]{2,1,0:T(8,128)S(1)} %get-tuple-element.7.rhs_ref), channel_id=1, replica_groups=mesh['ta'=4,'gz'=8,'xy'=8] {'xy'}, dimensions={0} | all-to-all | bytes 65536 | tf_op jit(solution)/shard_map/all_to_all | solution.py:287
  16.1 5.6 %collective-permute-start.3 = (f32[8,8,128]{2,1,0:T(8,128)S(1)}, f32[8,8,128]{2,1,0:T(8,128)S(1)}, u32[]{:S(2)}, u32[]{:S(2)}) collective-permute-start(f32[8,8,128]{2,1,0:T(8,128)S(1)} %all_to_all.15.field_ref.rhs_ref), channel_id=1, source_target_pairs={{8,16},{24,32},{40,48},{56,0},{16,8},{32,24},{48,40},{0,56},{9,17}... | collective-permute-start | bytes 98312 | tf_op jit(solution)/shard_map/ppermute | solution.py:282
  21.6 0.0 collective-permute-start.2
  21.6 3.2 %collective-permute-start.1 = (f32[8,8,128]{2,1,0:T(8,128)S(1)}, f32[8,8,128]{2,1,0:T(8,128)S(1)}, u32[]{:S(2)}, u32[]{:S(2)}) collective-permute-start(f32[8,8,128]{2,1,0:T(8,128)S(1)} %all_to_all.15.field_ref.rhs_ref), channel_id=1, source_target_pairs={{1,2},{3,4},{5,6},{7,64},{65,66},{67,68},{69,70},{71,128},{129,130... | collective-permute-start | bytes 98312 | tf_op jit(solution)/shard_map/ppermute | solution.py:282
  24.9 0.0 collective-permute-start
  24.9 0.8 %shard_map.51.center_ref = f32[8,16,128]{2,1,0:T(8,128)S(1)} custom-call(f32[8,8,128]{2,1,0:T(8,128)S(1)} %all_to_all.15.field_ref.rhs_ref, bf16[8,2,9,128,128]{4,3,2,1,0:T(8,128)(2,1)S(1)} %get-tuple-element.8.links_ref), custom_call_target="tpu_custom_call" | custom-call | flops 41943040 | bytes 3000000 | tf_op jit(solution)/shard_map/pallas_call | solution.py:18
  25.7 0.0 collective-permute-done.3.z1_ref
  25.7 0.0 collective-permute-done.2.z0_ref
  25.7 1.4 %collective-permute-done.1.t1_ref = f32[8,8,128]{2,1,0:T(8,128)S(1)} collective-permute-done((f32[8,8,128]{2,1,0:T(8,128)S(1)}, f32[8,8,128]{2,1,0:T(8,128)S(1)}, u32[]{:S(2)}, u32[]{:S(2)}) %collective-permute-start.1) | collective-permute-done | bytes 32800 | tf_op jit(solution)/shard_map/ppermute | solution.py:282
  27.1 1.1 %collective-permute-done.t0_ref = f32[8,8,128]{2,1,0:T(8,128)S(1)} collective-permute-done((f32[8,8,128]{2,1,0:T(8,128)S(1)}, f32[8,8,128]{2,1,0:T(8,128)S(1)}, u32[]{:S(2)}, u32[]{:S(2)}) %collective-permute-start) | collective-permute-done | bytes 32800 | tf_op jit(solution)/shard_map/ppermute | solution.py:282
  28.1 0.7 shard_map.52
  28.8 0.0 copy-done
  28.8 1.6 %collective-permute-start.7 = (f32[8,8,128]{2,1,0:T(8,128)S(1)}, f32[8,8,128]{2,1,0:T(8,128)S(1)}, u32[]{:S(2)}, u32[]{:S(2)}) collective-permute-start(f32[8,8,128]{2,1,0:T(8,128)S(1)} %get-tuple-element.9.field_ref.image_ref), channel_id=1, source_target_pairs={{8,16},{24,32},{40,48},{56,0},{16,8},{32,24},{48,40},{0,56},{9,17}... | collective-permute-start | bytes 98312 | tf_op jit(solution)/shard_map/ppermute | solution.py:282
  30.4 0.7 %collective-permute-start.6 = (f32[8,8,128]{2,1,0:T(8,128)S(1)}, f32[8,8,128]{2,1,0:T(8,128)S(1)}, u32[]{:S(2)}, u32[]{:S(2)}) collective-permute-start(f32[8,8,128]{2,1,0:T(8,128)S(1)} %get-tuple-element.9.field_ref.image_ref), channel_id=1, source_target_pairs={{0,8},{16,24},{32,40},{48,56},{8,0},{24,16},{40,32},{56,48},{1,9},... | collective-permute-start | bytes 98312 | tf_op jit(solution)/shard_map/ppermute | solution.py:282
  31.2 2.9 %collective-permute-start.5 = (f32[8,8,128]{2,1,0:T(8,128)S(1)}, f32[8,8,128]{2,1,0:T(8,128)S(1)}, u32[]{:S(2)}, u32[]{:S(2)}) collective-permute-start(f32[8,8,128]{2,1,0:T(8,128)S(1)} %get-tuple-element.9.field_ref.image_ref), channel_id=1, source_target_pairs={{1,2},{3,4},{5,6},{7,64},{65,66},{67,68},{69,70},{71,128},{129,130... | collective-permute-start | bytes 98312 | tf_op jit(solution)/shard_map/ppermute | solution.py:282
  34.1 0.0 collective-permute-start.4
  34.1 0.8 %shard_map.53.center_ref = f32[8,16,128]{2,1,0:T(8,128)S(1)} custom-call(f32[8,8,128]{2,1,0:T(8,128)S(1)} %get-tuple-element.9.field_ref.image_ref, bf16[8,2,9,128,128]{4,3,2,1,0:T(8,128)(2,1)S(1)} %get-tuple-element.8.links_ref), custom_call_target="tpu_custom_call" | custom-call | flops 41943040 | bytes 3000000 | tf_op jit(solution)/shard_map/pallas_call | solution.py:18
  34.8 0.0 collective-permute-done.7.z1_ref
  34.8 0.0 collective-permute-done.6.z0_ref
  34.9 1.8 %collective-permute-done.5.t1_ref = f32[8,8,128]{2,1,0:T(8,128)S(1)} collective-permute-done((f32[8,8,128]{2,1,0:T(8,128)S(1)}, f32[8,8,128]{2,1,0:T(8,128)S(1)}, u32[]{:S(2)}, u32[]{:S(2)}) %collective-permute-start.5) | collective-permute-done | bytes 32800 | tf_op jit(solution)/shard_map/ppermute | solution.py:282
  36.6 0.3 collective-permute-done.4.t0_ref
  37.0 0.8 %shard_map.54 = f32[8,32,128]{2,1,0:T(8,128)S(1)} custom-call(f32[8,16,128]{2,1,0:T(8,128)S(1)} %shard_map.53.center_ref, f32[8,8,128]{2,1,0:T(8,128)S(1)} %get-tuple-element.9.field_ref.image_ref, f32[8,8,128]{2,1,0:T(8,128)S(1)} %collective-permute-done.4.t0_ref, f32[8,8,128]{2,1,0:T(8,128)S(1)} %collective-permute-done.5.t1_ref, ...), custom_call_target="tpu_custom_call" | custom-call | flops 33554432 | bytes 2000000 | tf_op jit(solution)/shard_map/pallas_call | solution.py:18
  37.7 9.6 %all_to_all.16.packed_ref = f32[8,32,128]{2,1,0:T(8,128)S(1)} all-to-all(f32[8,32,128]{2,1,0:T(8,128)S(1)} %shard_map.54), channel_id=1, replica_groups=mesh['ta'=4,'gz'=8,'xy'=8] {'xy'}, dimensions={0} | all-to-all | bytes 262144 | tf_op jit(solution)/shard_map/all_to_all | solution.py:287
  47.3 0.6 shard_map.55
  47.9 7.3 %all-to-all-start.2 = ((f32[32,1,128]{2,1,0:T(1,128)}), f32[32,1,128]{2,1,0:T(1,128)S(1)}, u32[]{:S(2)}, u32[]{:S(2)}) async-start(f32[32,1,128]{2,1,0:T(1,128)} %shard_map.55), calls=%async_computation.2 | async-start | bytes 32768 | tf_op jit(solution)/shard_map/all_to_all | solution.py:287
  55.2 0.0 copy-start.1
  55.2 2.8 %copy-done.1 = bf16[8,2,2,2,32,1536]{5,4,3,2,1,0:T(8,128)(2,1)S(1)} copy-done((bf16[8,2,2,2,32,1536]{5,4,3,2,1,0:T(8,128)(2,1)S(1)}, bf16[8,2,2,2,32,1536]{5,4,3,2,1,0:T(8,128)(2,1)}, u32[]{:S(2)}) %copy-start.1) | copy-done | bytes 6291480
  58.0 2.2 %shard_map.56.basis_ref = f32[8,64,1536]{2,1,0:T(8,128)S(1)} custom-call(f32[8,32,128]{2,1,0:T(8,128)S(1)} %all_to_all.16.packed_ref, f32[8,8,128]{2,1,0:T(8,128)S(1)} %get-tuple-element.7.rhs_ref, bf16[8,2,2,2,32,1536]{5,4,3,2,1,0:T(8,128)(2,1)S(1)} %copy-done.1), custom_call_target="tpu_custom_call" | custom-call | flops 805306368 | bytes 10000000 | tf_op jit(solution)/shard_map/pallas_call | solution.py:18
  60.2 4.3 %all-to-all-done.2.sums_ref = f32[32,1,128]{2,1,0:T(1,128)S(1)} async-done(((f32[32,1,128]{2,1,0:T(1,128)}), f32[32,1,128]{2,1,0:T(1,128)S(1)}, u32[]{:S(2)}, u32[]{:S(2)}) %all-to-all-start.2) | async-done | bytes 16416 | tf_op jit(solution)/shard_map/all_to_all | solution.py:287
  64.5 1.8 %shard_map.57 = (bf16[4,8,1,1,2,2,2,1536]{7,6,5,4,3,2,1,0:T(2,128)(2,1)}, f32[4,8,1,1,2,128]{5,4,3,2,1,0:T(2,128)}) custom-call(f32[32,1,128]{2,1,0:T(1,128)S(1)} %all-to-all-done.2.sums_ref, f32[8,32,128]{2,1,0:T(8,128)S(1)} %all_to_all.16.packed_ref, f32[8,8,128]{2,1,0:T(8,128)S(1)} %get-tuple-element.7.rhs_ref, f32[8,64,1536]{2,1,0:T(8,128)S(1)} %shard_map.56.basis_ref), custom_call_target="tpu_custom_call" | custom-call | flops 2000000 | bytes 4000000 | tf_op jit(solution)/shard_map/pallas_call | solution.py:18
Async XLA Ops:
  5.3 23.5 %copy-start = (bf16[8,2,2,2,32,1536]{5,4,3,2,1,0:T(8,128)(2,1)}, bf16[8,2,2,2,32,1536]{5,4,3,2,1,0:T(8,128)(2,1)S(1)}, u32[]{:S(2)}) copy-start(bf16[8,2,2,2,32,1536]{5,4,3,2,1,0:T(8,128)(2,1)S(1)} %get-tuple-element.11.vectors_ref) | copy-start | bytes 18874372
  16.1 9.6 %collective-permute-start.3 = (f32[8,8,128]{2,1,0:T(8,128)S(1)}, f32[8,8,128]{2,1,0:T(8,128)S(1)}, u32[]{:S(2)}, u32[]{:S(2)}) collective-permute-start(f32[8,8,128]{2,1,0:T(8,128)S(1)} %all_to_all.15.field_ref.rhs_ref), channel_id=1, source_target_pairs={{8,16},{24,32},{40,48},{56,0},{16,8},{32,24},{48,40},{0,56},{9,17}... | collective-permute-start | bytes 98312 | tf_op jit(solution)/shard_map/ppermute | solution.py:282
  21.6 4.1 %collective-permute-start.2 = (f32[8,8,128]{2,1,0:T(8,128)S(1)}, f32[8,8,128]{2,1,0:T(8,128)S(1)}, u32[]{:S(2)}, u32[]{:S(2)}) collective-permute-start(f32[8,8,128]{2,1,0:T(8,128)S(1)} %all_to_all.15.field_ref.rhs_ref), channel_id=1, source_target_pairs={{0,8},{16,24},{32,40},{48,56},{8,0},{24,16},{40,32},{56,48},{1,9},... | collective-permute-start | bytes 98312 | tf_op jit(solution)/shard_map/ppermute | solution.py:282
  21.6 5.4 %collective-permute-start.1 = (f32[8,8,128]{2,1,0:T(8,128)S(1)}, f32[8,8,128]{2,1,0:T(8,128)S(1)}, u32[]{:S(2)}, u32[]{:S(2)}) collective-permute-start(f32[8,8,128]{2,1,0:T(8,128)S(1)} %all_to_all.15.field_ref.rhs_ref), channel_id=1, source_target_pairs={{1,2},{3,4},{5,6},{7,64},{65,66},{67,68},{69,70},{71,128},{129,130... | collective-permute-start | bytes 98312 | tf_op jit(solution)/shard_map/ppermute | solution.py:282
  24.9 3.3 %collective-permute-start = (f32[8,8,128]{2,1,0:T(8,128)S(1)}, f32[8,8,128]{2,1,0:T(8,128)S(1)}, u32[]{:S(2)}, u32[]{:S(2)}) collective-permute-start(f32[8,8,128]{2,1,0:T(8,128)S(1)} %all_to_all.15.field_ref.rhs_ref), channel_id=1, source_target_pairs={{0,1},{2,3},{4,5},{6,7},{64,65},{66,67},{68,69},{70,71},{128,129},... | collective-permute-start | bytes 98312 | tf_op jit(solution)/shard_map/ppermute | solution.py:282
  28.8 6.0 %collective-permute-start.7 = (f32[8,8,128]{2,1,0:T(8,128)S(1)}, f32[8,8,128]{2,1,0:T(8,128)S(1)}, u32[]{:S(2)}, u32[]{:S(2)}) collective-permute-start(f32[8,8,128]{2,1,0:T(8,128)S(1)} %get-tuple-element.9.field_ref.image_ref), channel_id=1, source_target_pairs={{8,16},{24,32},{40,48},{56,0},{16,8},{32,24},{48,40},{0,56},{9,17}... | collective-permute-start | bytes 98312 | tf_op jit(solution)/shard_map/ppermute | solution.py:282
  30.4 4.4 %collective-permute-start.6 = (f32[8,8,128]{2,1,0:T(8,128)S(1)}, f32[8,8,128]{2,1,0:T(8,128)S(1)}, u32[]{:S(2)}, u32[]{:S(2)}) collective-permute-start(f32[8,8,128]{2,1,0:T(8,128)S(1)} %get-tuple-element.9.field_ref.image_ref), channel_id=1, source_target_pairs={{0,8},{16,24},{32,40},{48,56},{8,0},{24,16},{40,32},{56,48},{1,9},... | collective-permute-start | bytes 98312 | tf_op jit(solution)/shard_map/ppermute | solution.py:282
  31.2 5.5 %collective-permute-start.5 = (f32[8,8,128]{2,1,0:T(8,128)S(1)}, f32[8,8,128]{2,1,0:T(8,128)S(1)}, u32[]{:S(2)}, u32[]{:S(2)}) collective-permute-start(f32[8,8,128]{2,1,0:T(8,128)S(1)} %get-tuple-element.9.field_ref.image_ref), channel_id=1, source_target_pairs={{1,2},{3,4},{5,6},{7,64},{65,66},{67,68},{69,70},{71,128},{129,130... | collective-permute-start | bytes 98312 | tf_op jit(solution)/shard_map/ppermute | solution.py:282
  34.1 2.9 %collective-permute-start.4 = (f32[8,8,128]{2,1,0:T(8,128)S(1)}, f32[8,8,128]{2,1,0:T(8,128)S(1)}, u32[]{:S(2)}, u32[]{:S(2)}) collective-permute-start(f32[8,8,128]{2,1,0:T(8,128)S(1)} %get-tuple-element.9.field_ref.image_ref), channel_id=1, source_target_pairs={{0,1},{2,3},{4,5},{6,7},{64,65},{66,67},{68,69},{70,71},{128,129},... | collective-permute-start | bytes 98312 | tf_op jit(solution)/shard_map/ppermute | solution.py:282
  47.9 16.5 %all-to-all-start.2 = ((f32[32,1,128]{2,1,0:T(1,128)}), f32[32,1,128]{2,1,0:T(1,128)S(1)}, u32[]{:S(2)}, u32[]{:S(2)}) async-start(f32[32,1,128]{2,1,0:T(1,128)} %shard_map.55), calls=%async_computation.2 | async-start | bytes 32768 | tf_op jit(solution)/shard_map/all_to_all | solution.py:287
  55.2 2.8 %copy-start.1 = (bf16[8,2,2,2,32,1536]{5,4,3,2,1,0:T(8,128)(2,1)S(1)}, bf16[8,2,2,2,32,1536]{5,4,3,2,1,0:T(8,128)(2,1)}, u32[]{:S(2)}) copy-start(bf16[8,2,2,2,32,1536]{5,4,3,2,1,0:T(8,128)(2,1)} %copy-done) | copy-start | bytes 18874372

commit v3 on v2

--- a/solution.py
+++ b/solution.py
@@ -8,9 +8,12 @@
 F32 = jnp.float32
 BF16 = jnp.bfloat16
 RHS = 4
-LIMIT = 52
+LIMIT = 56
+PARTS = 4
 ROWS = 8
 DOF = 128
+TIME = ("ta", "xy")
+EXCHANGES = ((TIME, 0), ("gz", 0), ("gz", 1), (TIME, 1))
 VMEM = pl.BlockSpec(memory_space=pltpu.VMEM)
 
 
@@ -18,7 +21,7 @@
     return pl.pallas_call(
         kernel,
         out_shape=out_shape,
-        in_specs=[inputs] * len(arguments),
+        in_specs=inputs if isinstance(inputs, list) else [inputs] * len(arguments),
         out_specs=outputs if outputs is not None else ([VMEM] * len(out_shape) if isinstance(out_shape, tuple) else VMEM),
         scratch_shapes=scratch,
         compiler_params=pltpu.CompilerParams(vmem_limit_bytes=limit * 1024 * 1024),
@@ -47,7 +50,7 @@
 
 
 def restrict_kernel(
-    source_hbm, vectors_hbm, links_hbm, out_ref, vectors, links, source, rows, full, source_sem, vectors_sem, links_sem
+    source_hbm, vectors_hbm, links_hbm, out_ref, links, vectors, source, rows, full, source_sem, vectors_sem, links_sem
 ):
     times = vectors.shape[0]
     half = times // 2
@@ -83,7 +86,7 @@
     def combine(group):
         for time in group:
             first, second = diagonal(time, 0), diagonal(time, 1)
-            out_ref[time] = jnp.where(
+            out_ref[turned(time, times)] = jnp.where(
                 real, first + pltpu.roll(second, 96, 1), pltpu.roll(second, 32, 1) - first
             )
 
@@ -111,7 +114,7 @@
 def blocks_of(links_ref, across, directions):
     return jnp.concatenate(
         [
-            jnp.concatenate([links_ref[across, along, d] for d in directions], axis=1)
+            jnp.concatenate([links_ref[turned(across), along, d] for d in directions], axis=1)
             for along in range(2)
         ],
         axis=0,
@@ -145,13 +148,14 @@
 
 def around_directions():
     time, depth = lax.axis_index("xy") % 2, lax.axis_index("gz") % 2
-    return (1 + time, 2 - time, 3 + depth, 4 - depth)
-
-
-def image_kernel(center_ref, field_ref, t0_ref, t1_ref, z0_ref, z1_ref, links_ref, image_ref, rest_ref):
+    numbers = {("ta", "xy"): (1 + time, 2 - time), "gz": (3 + depth, 4 - depth)}
+    return [numbers[axis][first] for axis, first in EXCHANGES]
+
+
+def image_kernel(center_ref, field_ref, a_ref, b_ref, c_ref, d_ref, links_ref, image_ref, rest_ref):
     directions = around_directions()
     for across in range(field_ref.shape[0]):
-        fields = [-ref[across] for ref in (t0_ref, t1_ref, z0_ref, z1_ref)]
+        fields = [-ref[across] for ref in (a_ref, b_ref, c_ref, d_ref)]
         hops = center_ref[across] + hop(links_ref, across, fields, directions)
         own = field_ref[across]
         rounded = own.astype(BF16).astype(F32)
@@ -163,12 +167,12 @@
 
 
 def second_kernel(
-    center_ref, image_ref, t0_ref, t1_ref, z0_ref, z1_ref, links_ref, rhs_ref, rest_ref, out_ref
+    center_ref, image_ref, a_ref, b_ref, c_ref, d_ref, links_ref, rhs_ref, rest_ref, out_ref
 ):
     directions = around_directions()
     totals = [jnp.zeros((ROWS, DOF), F32) for _ in PAIRS]
     for across in range(image_ref.shape[0]):
-        fields = [-ref[across] for ref in (t0_ref, t1_ref, z0_ref, z1_ref)]
+        fields = [-ref[across] for ref in (a_ref, b_ref, c_ref, d_ref)]
         hops = center_ref[across] + hop(links_ref, across, fields, directions)
         hops = hops[:ROWS] + hops[ROWS:]
         image, rest = image_ref[across], rest_ref[across]
@@ -212,17 +216,30 @@
     return jnp.concatenate(rows, axis=0)
 
 
-def basis_kernel(packed_ref, rhs_ref, vectors_ref, out_ref):
+def basis_kernel(packed_ref, rhs_ref, vectors_hbm, out_ref, vectors, sems):
+    times = vectors.shape[0]
+    part = times // PARTS
+    copies = []
+    for number in range(PARTS):
+        span = pl.ds(number * part, part)
+        copy = pltpu.make_async_copy(vectors_hbm.at[span, 0, 0], vectors.at[span], sems.at[number])
+        copy.start()
+        copies.append(copy)
     row, column = index((32, 32), 0), index((32, 32), 1)
     order = column == (row % 2) * 16 + ((row // 8) % 2) * 8 + (row // 16) * 4 + (row // 2) % 4
     order = jnp.where(order, 1.0, 0.0).astype(BF16)
-    for time in range(packed_ref.shape[0]):
-        parts = []
-        for field in (rhs_ref[time], packed_ref[time, 0:8]):
+    lefts = []
+    for time in range(times):
+        pieces = []
+        for field in (rhs_ref[turned(time)], packed_ref[turned(time), 0:8]):
             high = field.astype(BF16).astype(F32)
-            for part in (high, field - high):
-                parts.append(dot_nn(order, block_rows(part).astype(BF16)).astype(BF16))
-        fields = dot_nn(jnp.concatenate(parts, axis=0), vectors_ref[time].reshape(256, -1))
+            for piece in (high, field - high):
+                pieces.append(dot_nn(order, block_rows(piece).astype(BF16)).astype(BF16))
+        lefts.append(jnp.concatenate(pieces, axis=0))
+    for time in range(times):
+        if time % part == 0:
+            copies[time // part].wait()
+        fields = dot_nn(lefts[time], vectors[time].reshape(256, -1))
         out_ref[time, 0:32] = fields[0:32] + fields[32:64]
         out_ref[time, 32:64] = fields[64:96] + fields[96:128]
 
@@ -244,7 +261,9 @@
     return alpha_zero, alpha_one, gamma + kappa, kappa
 
 
-def finish_kernel(sums_ref, packed_ref, rhs_ref, basis_ref, correction_hbm, residual_ref, correction, sems):
+def finish_kernel(
+    sums_ref, packed_ref, rhs_ref, basis_ref, correction_hbm, residual_hbm, correction, residual, sems, residual_sem
+):
     times = packed_ref.shape[0]
     total = jnp.sum(sums_ref[...], axis=0)
     alpha_zero, alpha_one, beta, kappa = coefficients(total, (index((32, DOF), 0) // 2) % RHS)
@@ -261,30 +280,43 @@
         copy = pltpu.make_async_copy(correction.at[:, time], correction_hbm.at[:, time], sems.at[time])
         copy.start()
         copies.append(copy)
-    alpha_zero, alpha_one, beta, kappa = coefficients(total, index((ROWS, DOF), 0) % RHS)
-    for time in range(times):
-        image, rest, hops = (packed_ref[time, i : i + 8] for i in (0, 8, 16))
-        residual = rhs_ref[time] - (alpha_zero - alpha_one * kappa) * image
-        residual = residual - alpha_one * (rest - alpha_zero * hops)
-        for r in range(RHS):
-            for y in range(2):
-                residual_ref[r, time, 0, 0, y : y + 1] = residual[y * RHS + r : y * RHS + r + 1]
+        if time == 0:
+            alpha_zero, alpha_one, beta, kappa = coefficients(total, index((ROWS, DOF), 0) % RHS)
+            for t in range(times):
+                image, rest, hops = (packed_ref[turned(t), i : i + 8] for i in (0, 8, 16))
+                value = rhs_ref[turned(t)] - (alpha_zero - alpha_one * kappa) * image
+                value = value - alpha_one * (rest - alpha_zero * hops)
+                for r in range(RHS):
+                    for y in range(2):
+                        residual[r, t, 0, 0, y : y + 1] = value[y * RHS + r : y * RHS + r + 1]
+            copy = pltpu.make_async_copy(residual, residual_hbm, residual_sem)
+            copy.start()
+            copies.append(copy)
     for copy in copies:
         copy.wait()
 
 
 def neighbours(field):
     found = []
-    for axis in (("ta", "xy"), "gz"):
+    for axis, first in EXCHANGES:
         devices = lax.axis_size(axis)
-        for first in range(2):
-            pairs = [(i, (i + 1) % devices) for i in range(first, devices, 2)]
-            found.append(lax.ppermute(field, axis, pairs + [(j, i) for i, j in pairs]))
+        pairs = [(i, (i + 1) % devices) for i in range(first, devices, 2)]
+        found.append(lax.ppermute(field, axis, pairs + [(j, i) for i, j in pairs]))
     return found
 
 
-def exchange(array, axis):
-    return lax.all_to_all(array, axis, split_axis=0, concat_axis=0, tiled=True)
+def turned(number, devices=8):
+    return (number + devices // 2) % devices
+
+
+def far_first():
+    depth = lax.axis_size("gz")
+    devices = lax.axis_size("ta") * depth
+    return [[(devices // 2 + depth // 2 + i) % devices for i in range(devices)]]
+
+
+def exchange(array, axis, groups=None):
+    return lax.all_to_all(array, axis, split_axis=0, concat_axis=0, tiled=True, axis_index_groups=groups)
 
 
 def body(fine_source, vectors, coarse_links):
@@ -295,11 +327,11 @@
     length = vectors.shape[-1]
 
     anywhere = pl.BlockSpec(memory_space=pl.ANY)
-    fine_rhs, vectors, links = call(
+    local_vectors = pltpu.VMEM(vectors.shape[:1] + vectors.shape[3:], BF16)
+    fine_rhs, links = call(
         restrict_kernel,
         (
             shape(times, ROWS, DOF),
-            shape(*vectors.shape[:1], *vectors.shape[3:], dtype=BF16),
             shape(*coarse_links.shape[2:], dtype=BF16),
         ),
         (fine_source, vectors, coarse_links),
@@ -307,6 +339,7 @@
         12_000_000,
         inputs=anywhere,
         scratch=[
+            local_vectors,
             pltpu.VMEM(fine_source.shape, BF16),
             pltpu.VMEM((times, 32, length), BF16),
             pltpu.VMEM((times, 2, 32, DOF), F32),
@@ -316,7 +349,8 @@
         ],
         limit=LIMIT,
     )
-    rhs = exchange(fine_rhs, "xy")
+    halfway = [[turned(i, sites) for i in range(sites)]]
+    rhs = exchange(fine_rhs, "xy", halfway)
     around = neighbours(rhs)
     center = call(center_kernel, shape(*doubled), (rhs, links), 2 * sites * 5 * 16 * 256 * 128, 3_000_000)
     image, rest = call(
@@ -335,17 +369,20 @@
         2 * sites * 4 * 16 * 256 * 128,
         2_000_000,
     )
-    packed = exchange(packed, "xy")
+    packed = exchange(packed, "xy", halfway)
     sums = call(
         sums_kernel, shape(lax.axis_size("ta") * lax.axis_size("gz"), 1, DOF), (packed,), 10_000, 50_000
     )
-    sums = exchange(sums, ("ta", "gz"))
+    sums = exchange(sums, ("ta", "gz"), far_first())
     basis = call(
         basis_kernel,
         shape(times, 64, length),
-        (packed, fine_rhs, vectors),
+        (packed, fine_rhs, pltpu.with_memory_space_constraint(vectors, pltpu.HBM)),
         2 * times * 128 * 256 * length,
         10_000_000,
+        inputs=[VMEM, VMEM, anywhere],
+        scratch=[local_vectors, pltpu.SemaphoreType.DMA((PARTS,))],
+        limit=24,
     )
     correction, residual = call(
         finish_kernel,
@@ -356,8 +393,13 @@
         (sums, packed, fine_rhs, basis),
         2_000_000,
         4_000_000,
-        outputs=(anywhere, VMEM),
-        scratch=[pltpu.VMEM(fine_source.shape, BF16), pltpu.SemaphoreType.DMA((times,))],
+        outputs=(anywhere, anywhere),
+        scratch=[
+            pltpu.VMEM(fine_source.shape, BF16),
+            pltpu.VMEM((RHS, times, 1, 1, 2, DOF), F32),
+            pltpu.SemaphoreType.DMA((times,)),
+            pltpu.SemaphoreType.DMA,
+        ],
     )
     return (correction, residual)
 

time: 66.6 us -> 61.3 us (0.920)
  starting transfers between devices: 21.4 us -> 26.6 us
  waiting for transfers between devices: 8.93 us -> 4.27 us
  blocking collectives: 20.3 us -> 16.8 us
  local copies, waits for them, and re-layouts: 2.78 us -> 0 us
    all_to_all x1, starting transfers between devices: 7.26 us -> 12.6 us  [exchange(): lax.all_to_all(array, axis, split_axis=0, concat_axis=0, tiled=True, axis...]
    all_to_all x1, waiting for transfers between devices: 4.33 us -> 0.01 us  [exchange(): lax.all_to_all(array, axis, split_axis=0, concat_axis=0, tiled=True, axis...]
    all_to_all x2, blocking collectives: 20.3 us -> 16.8 us  [exchange(): lax.all_to_all(array, axis, split_axis=0, concat_axis=0, tiled=True, axis...]
    unnamed x4 -> x0, local copies, waits for them, and re-layouts: 2.78 us -> none
  transfers between devices with their start and end apart: 9 -> 9, of which waited for: 5 -> 6; matrix products, arithmetic and copies ran while one was open for 0% -> 0% of each run, Pallas kernels for 6% -> 8%
where the time goes in v3:
time: 61.3 us; the launch traced here: 61.1 us
  starting transfers between devices  26.6 us (43%)
  blocking collectives  16.8 us (27%)
  Pallas kernels  12.8 us (21%)
  waiting for transfers between devices  4.27 us (7%)
  between operations  0.68 us (1%)
    all_to_all x2, blocking collectives, exchange(): lax.all_to_all(array, axis, split_axis=0, concat_axis=0, tiled=True, axis...  16.8 us
    ppermute x8, starting transfers between devices, neighbours(): found.append(lax.ppermute(field, axis, pairs + [(j, i) for i, j in pairs]))  13.9 us
    pallas_call x8, Pallas kernels, call(): pl.pallas_call(kernel, out_shape=out_shape, in_specs=inputs if isinstance...  12.8 us
    all_to_all x1, starting transfers between devices, exchange(): lax.all_to_all(array, axis, split_axis=0, concat_axis=0, tiled=True, axis...  12.6 us
    ppermute x8, waiting for transfers between devices, neighbours(): found.append(lax.ppermute(field, axis, pairs + [(j, i) for i, j in pairs]))  4.26 us
  transfers between devices with their start and end apart: 9, of which 6 were waited for; matrix products, arithmetic and copies ran while one was open for 0% of the time, Pallas kernels for 8%

profile of v3, /device:TPU:1, one launch (start us, length us, event | category | flops | bytes accessed | tf_op | source)
XLA Modules:
  0.0 61.1 jit_solution(17374682580126715722)
XLA Ops:
  0.6 4.6 %shard_map.50 = (f32[8,8,128]{2,1,0:T(8,128)S(1)}, bf16[8,2,9,128,128]{4,3,2,1,0:T(8,128)(2,1)S(1)}) custom-call(bf16[4,8,1,1,2,2,2,1536]{7,6,5,4,3,2,1,0:T(2,128)(2,1)} %source_hbm.1, bf16[8,1,1,2,2,2,32,1536]{7,6,5,4,3,2,1,0:T(8,128)(2,1)} %vectors_hbm.3, bf16[1,1,8,2,9,128,128]{6,5,4,3,2,1,0:T(8,128)(2,1)} %links_hbm.1), custom_call_target="tpu_custom_call" | custom-call | flops 201326592 | bytes 12000000 | tf_op jit(solution)/shard_map/pallas_call | solution.py:21
  5.3 9.3 %all_to_all.15.field_ref.rhs_ref = f32[8,8,128]{2,1,0:T(8,128)S(1)} all-to-all(f32[8,8,128]{2,1,0:T(8,128)S(1)} %get-tuple-element.6.rhs_ref), channel_id=1, replica_groups={{4,5,6,7,0,1,2,3},{12,13,14,15,8,9,10,11},{20,21,22,23,16,17,18,19},{28..., dimensions={0} | all-to-all | bytes 65536 | tf_op jit(solution)/shard_map/all_to_all | solution.py:319
  14.6 4.0 %collective-permute-start.3 = (f32[8,8,128]{2,1,0:T(8,128)S(1)}, f32[8,8,128]{2,1,0:T(8,128)S(1)}, u32[]{:S(2)}, u32[]{:S(2)}) collective-permute-start(f32[8,8,128]{2,1,0:T(8,128)S(1)} %all_to_all.15.field_ref.rhs_ref), channel_id=1, source_target_pairs={{1,2},{3,4},{5,6},{7,64},{65,66},{67,68},{69,70},{71,128},{129,130... | collective-permute-start | bytes 98312 | tf_op jit(solution)/shard_map/ppermute | solution.py:304
  18.6 5.5 %collective-permute-start.2 = (f32[8,8,128]{2,1,0:T(8,128)S(1)}, f32[8,8,128]{2,1,0:T(8,128)S(1)}, u32[]{:S(2)}, u32[]{:S(2)}) collective-permute-start(f32[8,8,128]{2,1,0:T(8,128)S(1)} %all_to_all.15.field_ref.rhs_ref), channel_id=1, source_target_pairs={{8,16},{24,32},{40,48},{56,0},{16,8},{32,24},{48,40},{0,56},{9,17}... | collective-permute-start | bytes 98312 | tf_op jit(solution)/shard_map/ppermute | solution.py:304
  24.2 0.0 collective-permute-start.1
  24.2 0.0 collective-permute-start
  24.2 0.8 %shard_map.51.center_ref = f32[8,16,128]{2,1,0:T(8,128)S(1)} custom-call(f32[8,8,128]{2,1,0:T(8,128)S(1)} %all_to_all.15.field_ref.rhs_ref, bf16[8,2,9,128,128]{4,3,2,1,0:T(8,128)(2,1)S(1)} %get-tuple-element.7.links_ref), custom_call_target="tpu_custom_call" | custom-call | flops 41943040 | bytes 3000000 | tf_op jit(solution)/shard_map/pallas_call | solution.py:21
  25.0 0.0 collective-permute-done.3.d_ref
  25.0 0.8 %collective-permute-done.2.c_ref = f32[8,8,128]{2,1,0:T(8,128)S(1)} collective-permute-done((f32[8,8,128]{2,1,0:T(8,128)S(1)}, f32[8,8,128]{2,1,0:T(8,128)S(1)}, u32[]{:S(2)}, u32[]{:S(2)}) %collective-permute-start.2) | collective-permute-done | bytes 32800 | tf_op jit(solution)/shard_map/ppermute | solution.py:304
  25.8 1.1 %collective-permute-done.1.b_ref = f32[8,8,128]{2,1,0:T(8,128)S(1)} collective-permute-done((f32[8,8,128]{2,1,0:T(8,128)S(1)}, f32[8,8,128]{2,1,0:T(8,128)S(1)}, u32[]{:S(2)}, u32[]{:S(2)}) %collective-permute-start.1) | collective-permute-done | bytes 32800 | tf_op jit(solution)/shard_map/ppermute | solution.py:304
  27.0 0.0 collective-permute-done.a_ref
  27.0 0.7 %shard_map.52 = (f32[8,8,128]{2,1,0:T(8,128)S(1)}, f32[8,8,128]{2,1,0:T(8,128)S(1)}) custom-call(f32[8,16,128]{2,1,0:T(8,128)S(1)} %shard_map.51.center_ref, f32[8,8,128]{2,1,0:T(8,128)S(1)} %all_to_all.15.field_ref.rhs_ref, f32[8,8,128]{2,1,0:T(8,128)S(1)} %collective-permute-done.a_ref, f32[8,8,128]{2,1,0:T(8,128)S(1)} %collective-permute-done.1.b_ref, ...), custom_call_target="tpu_custom_call" | custom-call | flops 33554432 | bytes 2000000 | tf_op jit(solution)/shard_map/pallas_call | solution.py:21
  27.6 1.9 %collective-permute-start.7 = (f32[8,8,128]{2,1,0:T(8,128)S(1)}, f32[8,8,128]{2,1,0:T(8,128)S(1)}, u32[]{:S(2)}, u32[]{:S(2)}) collective-permute-start(f32[8,8,128]{2,1,0:T(8,128)S(1)} %get-tuple-element.8.field_ref.image_ref), channel_id=1, source_target_pairs={{1,2},{3,4},{5,6},{7,64},{65,66},{67,68},{69,70},{71,128},{129,130... | collective-permute-start | bytes 98312 | tf_op jit(solution)/shard_map/ppermute | solution.py:304
  29.5 1.7 %collective-permute-start.6 = (f32[8,8,128]{2,1,0:T(8,128)S(1)}, f32[8,8,128]{2,1,0:T(8,128)S(1)}, u32[]{:S(2)}, u32[]{:S(2)}) collective-permute-start(f32[8,8,128]{2,1,0:T(8,128)S(1)} %get-tuple-element.8.field_ref.image_ref), channel_id=1, source_target_pairs={{8,16},{24,32},{40,48},{56,0},{16,8},{32,24},{48,40},{0,56},{9,17}... | collective-permute-start | bytes 98312 | tf_op jit(solution)/shard_map/ppermute | solution.py:304
  31.2 0.7 %collective-permute-start.5 = (f32[8,8,128]{2,1,0:T(8,128)S(1)}, f32[8,8,128]{2,1,0:T(8,128)S(1)}, u32[]{:S(2)}, u32[]{:S(2)}) collective-permute-start(f32[8,8,128]{2,1,0:T(8,128)S(1)} %get-tuple-element.8.field_ref.image_ref), channel_id=1, source_target_pairs={{0,8},{16,24},{32,40},{48,56},{8,0},{24,16},{40,32},{56,48},{1,9},... | collective-permute-start | bytes 98312 | tf_op jit(solution)/shard_map/ppermute | solution.py:304
  32.0 0.0 collective-permute-start.4
  32.0 0.8 %shard_map.53.center_ref = f32[8,16,128]{2,1,0:T(8,128)S(1)} custom-call(f32[8,8,128]{2,1,0:T(8,128)S(1)} %get-tuple-element.8.field_ref.image_ref, bf16[8,2,9,128,128]{4,3,2,1,0:T(8,128)(2,1)S(1)} %get-tuple-element.7.links_ref), custom_call_target="tpu_custom_call" | custom-call | flops 41943040 | bytes 3000000 | tf_op jit(solution)/shard_map/pallas_call | solution.py:21
  32.7 0.4 collective-permute-done.7.d_ref
  33.2 0.3 collective-permute-done.6.c_ref
  33.5 0.8 %collective-permute-done.5.b_ref = f32[8,8,128]{2,1,0:T(8,128)S(1)} collective-permute-done((f32[8,8,128]{2,1,0:T(8,128)S(1)}, f32[8,8,128]{2,1,0:T(8,128)S(1)}, u32[]{:S(2)}, u32[]{:S(2)}) %collective-permute-start.5) | collective-permute-done | bytes 32800 | tf_op jit(solution)/shard_map/ppermute | solution.py:304
  34.3 0.7 %collective-permute-done.4.a_ref = f32[8,8,128]{2,1,0:T(8,128)S(1)} collective-permute-done((f32[8,8,128]{2,1,0:T(8,128)S(1)}, f32[8,8,128]{2,1,0:T(8,128)S(1)}, u32[]{:S(2)}, u32[]{:S(2)}) %collective-permute-start.4) | collective-permute-done | bytes 32800 | tf_op jit(solution)/shard_map/ppermute | solution.py:304
  35.0 0.8 %shard_map.54 = f32[8,32,128]{2,1,0:T(8,128)S(1)} custom-call(f32[8,16,128]{2,1,0:T(8,128)S(1)} %shard_map.53.center_ref, f32[8,8,128]{2,1,0:T(8,128)S(1)} %get-tuple-element.8.field_ref.image_ref, f32[8,8,128]{2,1,0:T(8,128)S(1)} %collective-permute-done.4.a_ref, f32[8,8,128]{2,1,0:T(8,128)S(1)} %collective-permute-done.5.b_ref, ...), custom_call_target="tpu_custom_call" | custom-call | flops 33554432 | bytes 2000000 | tf_op jit(solution)/shard_map/pallas_call | solution.py:21
  35.8 7.5 %all_to_all.16.packed_ref = f32[8,32,128]{2,1,0:T(8,128)S(1)} all-to-all(f32[8,32,128]{2,1,0:T(8,128)S(1)} %shard_map.54), channel_id=1, replica_groups={{4,5,6,7,0,1,2,3},{12,13,14,15,8,9,10,11},{20,21,22,23,16,17,18,19},{28..., dimensions={0} | all-to-all | bytes 262144 | tf_op jit(solution)/shard_map/all_to_all | solution.py:319
  43.3 0.6 %shard_map.55 = f32[32,1,128]{2,1,0:T(1,128)} custom-call(f32[8,32,128]{2,1,0:T(8,128)S(1)} %all_to_all.16.packed_ref), custom_call_target="tpu_custom_call" | custom-call | flops 10000 | bytes 50000 | tf_op jit(solution)/shard_map/pallas_call | solution.py:21
  43.9 12.6 %all-to-all-start.2 = ((f32[32,1,128]{2,1,0:T(1,128)}), f32[32,1,128]{2,1,0:T(1,128)S(1)}, u32[]{:S(2)}, u32[]{:S(2)}) async-start(f32[32,1,128]{2,1,0:T(1,128)} %shard_map.55), calls=%async_computation.2 | async-start | bytes 32768 | tf_op jit(solution)/shard_map/all_to_all | solution.py:319
  56.5 3.3 %shard_map.56.basis_ref = f32[8,64,1536]{2,1,0:T(8,128)S(1)} custom-call(f32[8,32,128]{2,1,0:T(8,128)S(1)} %all_to_all.16.packed_ref, f32[8,8,128]{2,1,0:T(8,128)S(1)} %get-tuple-element.6.rhs_ref, bf16[8,1,1,2,2,2,32,1536]{7,6,5,4,3,2,1,0:T(8,128)(2,1)} %vectors_hbm.3), custom_call_target="tpu_custom_call" | custom-call | flops 805306368 | bytes 10000000 | tf_op jit(solution)/shard_map/pallas_call | solution.py:21
  59.8 0.0 all-to-all-done.2.sums_ref
  59.8 1.2 %shard_map.57 = (bf16[4,8,1,1,2,2,2,1536]{7,6,5,4,3,2,1,0:T(2,128)(2,1)}, f32[4,8,1,1,2,128]{5,4,3,2,1,0:T(2,128)}) custom-call(f32[32,1,128]{2,1,0:T(1,128)S(1)} %all-to-all-done.2.sums_ref, f32[8,32,128]{2,1,0:T(8,128)S(1)} %all_to_all.16.packed_ref, f32[8,8,128]{2,1,0:T(8,128)S(1)} %get-tuple-element.6.rhs_ref, f32[8,64,1536]{2,1,0:T(8,128)S(1)} %shard_map.56.basis_ref), custom_call_target="tpu_custom_call" | custom-call | flops 2000000 | bytes 4000000 | tf_op jit(solution)/shard_map/pallas_call | solution.py:21
Async XLA Ops:
  14.6 10.4 %collective-permute-start.3 = (f32[8,8,128]{2,1,0:T(8,128)S(1)}, f32[8,8,128]{2,1,0:T(8,128)S(1)}, u32[]{:S(2)}, u32[]{:S(2)}) collective-permute-start(f32[8,8,128]{2,1,0:T(8,128)S(1)} %all_to_all.15.field_ref.rhs_ref), channel_id=1, source_target_pairs={{1,2},{3,4},{5,6},{7,64},{65,66},{67,68},{69,70},{71,128},{129,130... | collective-permute-start | bytes 98312 | tf_op jit(solution)/shard_map/ppermute | solution.py:304
  18.6 7.2 %collective-permute-start.2 = (f32[8,8,128]{2,1,0:T(8,128)S(1)}, f32[8,8,128]{2,1,0:T(8,128)S(1)}, u32[]{:S(2)}, u32[]{:S(2)}) collective-permute-start(f32[8,8,128]{2,1,0:T(8,128)S(1)} %all_to_all.15.field_ref.rhs_ref), channel_id=1, source_target_pairs={{8,16},{24,32},{40,48},{56,0},{16,8},{32,24},{48,40},{0,56},{9,17}... | collective-permute-start | bytes 98312 | tf_op jit(solution)/shard_map/ppermute | solution.py:304
  24.2 2.8 %collective-permute-start.1 = (f32[8,8,128]{2,1,0:T(8,128)S(1)}, f32[8,8,128]{2,1,0:T(8,128)S(1)}, u32[]{:S(2)}, u32[]{:S(2)}) collective-permute-start(f32[8,8,128]{2,1,0:T(8,128)S(1)} %all_to_all.15.field_ref.rhs_ref), channel_id=1, source_target_pairs={{0,8},{16,24},{32,40},{48,56},{8,0},{24,16},{40,32},{56,48},{1,9},... | collective-permute-start | bytes 98312 | tf_op jit(solution)/shard_map/ppermute | solution.py:304
  24.2 2.8 %collective-permute-start = (f32[8,8,128]{2,1,0:T(8,128)S(1)}, f32[8,8,128]{2,1,0:T(8,128)S(1)}, u32[]{:S(2)}, u32[]{:S(2)}) collective-permute-start(f32[8,8,128]{2,1,0:T(8,128)S(1)} %all_to_all.15.field_ref.rhs_ref), channel_id=1, source_target_pairs={{0,1},{2,3},{4,5},{6,7},{64,65},{66,67},{68,69},{70,71},{128,129},... | collective-permute-start | bytes 98312 | tf_op jit(solution)/shard_map/ppermute | solution.py:304
  27.6 5.5 %collective-permute-start.7 = (f32[8,8,128]{2,1,0:T(8,128)S(1)}, f32[8,8,128]{2,1,0:T(8,128)S(1)}, u32[]{:S(2)}, u32[]{:S(2)}) collective-permute-start(f32[8,8,128]{2,1,0:T(8,128)S(1)} %get-tuple-element.8.field_ref.image_ref), channel_id=1, source_target_pairs={{1,2},{3,4},{5,6},{7,64},{65,66},{67,68},{69,70},{71,128},{129,130... | collective-permute-start | bytes 98312 | tf_op jit(solution)/shard_map/ppermute | solution.py:304
  29.5 4.0 %collective-permute-start.6 = (f32[8,8,128]{2,1,0:T(8,128)S(1)}, f32[8,8,128]{2,1,0:T(8,128)S(1)}, u32[]{:S(2)}, u32[]{:S(2)}) collective-permute-start(f32[8,8,128]{2,1,0:T(8,128)S(1)} %get-tuple-element.8.field_ref.image_ref), channel_id=1, source_target_pairs={{8,16},{24,32},{40,48},{56,0},{16,8},{32,24},{48,40},{0,56},{9,17}... | collective-permute-start | bytes 98312 | tf_op jit(solution)/shard_map/ppermute | solution.py:304
  31.2 3.1 %collective-permute-start.5 = (f32[8,8,128]{2,1,0:T(8,128)S(1)}, f32[8,8,128]{2,1,0:T(8,128)S(1)}, u32[]{:S(2)}, u32[]{:S(2)}) collective-permute-start(f32[8,8,128]{2,1,0:T(8,128)S(1)} %get-tuple-element.8.field_ref.image_ref), channel_id=1, source_target_pairs={{0,8},{16,24},{32,40},{48,56},{8,0},{24,16},{40,32},{56,48},{1,9},... | collective-permute-start | bytes 98312 | tf_op jit(solution)/shard_map/ppermute | solution.py:304
  32.0 3.1 %collective-permute-start.4 = (f32[8,8,128]{2,1,0:T(8,128)S(1)}, f32[8,8,128]{2,1,0:T(8,128)S(1)}, u32[]{:S(2)}, u32[]{:S(2)}) collective-permute-start(f32[8,8,128]{2,1,0:T(8,128)S(1)} %get-tuple-element.8.field_ref.image_ref), channel_id=1, source_target_pairs={{0,1},{2,3},{4,5},{6,7},{64,65},{66,67},{68,69},{70,71},{128,129},... | collective-permute-start | bytes 98312 | tf_op jit(solution)/shard_map/ppermute | solution.py:304
  43.9 15.9 %all-to-all-start.2 = ((f32[32,1,128]{2,1,0:T(1,128)}), f32[32,1,128]{2,1,0:T(1,128)S(1)}, u32[]{:S(2)}, u32[]{:S(2)}) async-start(f32[32,1,128]{2,1,0:T(1,128)} %shard_map.55), calls=%async_computation.2 | async-start | bytes 32768 | tf_op jit(solution)/shard_map/all_to_all | solution.py:319

commit v4 on v3

--- a/solution.py
+++ b/solution.py
@@ -10,6 +10,8 @@
 RHS = 4
 LIMIT = 56
 PARTS = 4
+TURN = 4
+FIRST = (3, 6)
 ROWS = 8
 DOF = 128
 TIME = ("ta", "xy")
@@ -86,7 +88,7 @@
     def combine(group):
         for time in group:
             first, second = diagonal(time, 0), diagonal(time, 1)
-            out_ref[turned(time, times)] = jnp.where(
+            out_ref[place_of(time, times)] = jnp.where(
                 real, first + pltpu.roll(second, 96, 1), pltpu.roll(second, 32, 1) - first
             )
 
@@ -231,7 +233,7 @@
     lefts = []
     for time in range(times):
         pieces = []
-        for field in (rhs_ref[turned(time)], packed_ref[turned(time), 0:8]):
+        for field in (rhs_ref[place_of(time)], packed_ref[place_of(time), 0:8]):
             high = field.astype(BF16).astype(F32)
             for piece in (high, field - high):
                 pieces.append(dot_nn(order, block_rows(piece).astype(BF16)).astype(BF16))
@@ -283,8 +285,8 @@
         if time == 0:
             alpha_zero, alpha_one, beta, kappa = coefficients(total, index((ROWS, DOF), 0) % RHS)
             for t in range(times):
-                image, rest, hops = (packed_ref[turned(t), i : i + 8] for i in (0, 8, 16))
-                value = rhs_ref[turned(t)] - (alpha_zero - alpha_one * kappa) * image
+                image, rest, hops = (packed_ref[place_of(t), i : i + 8] for i in (0, 8, 16))
+                value = rhs_ref[place_of(t)] - (alpha_zero - alpha_one * kappa) * image
                 value = value - alpha_one * (rest - alpha_zero * hops)
                 for r in range(RHS):
                     for y in range(2):
@@ -305,14 +307,18 @@
     return found
 
 
-def turned(number, devices=8):
-    return (number + devices // 2) % devices
+def turned(place, devices=8):
+    return (place + TURN) % devices
+
+
+def place_of(number, devices=8):
+    return (number - TURN) % devices
 
 
 def far_first():
     depth = lax.axis_size("gz")
     devices = lax.axis_size("ta") * depth
-    return [[(devices // 2 + depth // 2 + i) % devices for i in range(devices)]]
+    return [[(FIRST[0] * depth + FIRST[1] + i) % devices for i in range(devices)]]
 
 
 def exchange(array, axis, groups=None):

time: 61.3 us -> 60.6 us (0.989)
  starting transfers between devices: 26.6 us -> 25.4 us
    all_to_all x1, starting transfers between devices: 12.6 us -> 11.5 us  [exchange(): lax.all_to_all(array, axis, split_axis=0, concat_axis=0, tiled=True, axis...]
  transfers between devices with their start and end apart: 9 -> 9, of which waited for: 6 -> 7; matrix products, arithmetic and copies ran while one was open for 0% -> 0% of each run, Pallas kernels for 8% -> 8%
where the time goes in v4:
time: 60.6 us; the launch traced here: 60.4 us
  starting transfers between devices  25.4 us (42%)
  blocking collectives  16.8 us (28%)
  Pallas kernels  12.8 us (21%)
  waiting for transfers between devices  4.74 us (8%)
  between operations  0.67 us (1%)
    all_to_all x2, blocking collectives, exchange(): lax.all_to_all(array, axis, split_axis=0, concat_axis=0, tiled=True, axis...  16.8 us
    ppermute x8, starting transfers between devices, neighbours(): found.append(lax.ppermute(field, axis, pairs + [(j, i) for i, j in pairs]))  13.9 us
    pallas_call x8, Pallas kernels, call(): pl.pallas_call(kernel, out_shape=out_shape, in_specs=inputs if isinstance...  12.8 us
    all_to_all x1, starting transfers between devices, exchange(): lax.all_to_all(array, axis, split_axis=0, concat_axis=0, tiled=True, axis...  11.5 us
    ppermute x8, waiting for transfers between devices, neighbours(): found.append(lax.ppermute(field, axis, pairs + [(j, i) for i, j in pairs]))  4.26 us
  transfers between devices with their start and end apart: 9, of which 7 were waited for; matrix products, arithmetic and copies ran while one was open for 0% of the time, Pallas kernels for 8%

profile of v4, /device:TPU:1, one launch (start us, length us, event | category | flops | bytes accessed | tf_op | source)
XLA Modules:
  0.0 60.4 jit_solution(5555137422855727351)
XLA Ops:
  0.6 4.6 %shard_map.50 = (f32[8,8,128]{2,1,0:T(8,128)S(1)}, bf16[8,2,9,128,128]{4,3,2,1,0:T(8,128)(2,1)S(1)}) custom-call(bf16[4,8,1,1,2,2,2,1536]{7,6,5,4,3,2,1,0:T(2,128)(2,1)} %source_hbm.1, bf16[8,1,1,2,2,2,32,1536]{7,6,5,4,3,2,1,0:T(8,128)(2,1)} %vectors_hbm.3, bf16[1,1,8,2,9,128,128]{6,5,4,3,2,1,0:T(8,128)(2,1)} %links_hbm.1), custom_call_target="tpu_custom_call" | custom-call | flops 201326592 | bytes 12000000 | tf_op jit(solution)/shard_map/pallas_call | solution.py:23
  5.3 9.3 %all_to_all.15.field_ref.rhs_ref = f32[8,8,128]{2,1,0:T(8,128)S(1)} all-to-all(f32[8,8,128]{2,1,0:T(8,128)S(1)} %get-tuple-element.6.rhs_ref), channel_id=1, replica_groups={{4,5,6,7,0,1,2,3},{12,13,14,15,8,9,10,11},{20,21,22,23,16,17,18,19},{28..., dimensions={0} | all-to-all | bytes 65536 | tf_op jit(solution)/shard_map/all_to_all | solution.py:325
  14.6 4.0 %collective-permute-start.3 = (f32[8,8,128]{2,1,0:T(8,128)S(1)}, f32[8,8,128]{2,1,0:T(8,128)S(1)}, u32[]{:S(2)}, u32[]{:S(2)}) collective-permute-start(f32[8,8,128]{2,1,0:T(8,128)S(1)} %all_to_all.15.field_ref.rhs_ref), channel_id=1, source_target_pairs={{1,2},{3,4},{5,6},{7,64},{65,66},{67,68},{69,70},{71,128},{129,130... | collective-permute-start | bytes 98312 | tf_op jit(solution)/shard_map/ppermute | solution.py:306
  18.6 5.5 %collective-permute-start.2 = (f32[8,8,128]{2,1,0:T(8,128)S(1)}, f32[8,8,128]{2,1,0:T(8,128)S(1)}, u32[]{:S(2)}, u32[]{:S(2)}) collective-permute-start(f32[8,8,128]{2,1,0:T(8,128)S(1)} %all_to_all.15.field_ref.rhs_ref), channel_id=1, source_target_pairs={{8,16},{24,32},{40,48},{56,0},{16,8},{32,24},{48,40},{0,56},{9,17}... | collective-permute-start | bytes 98312 | tf_op jit(solution)/shard_map/ppermute | solution.py:306
  24.2 0.0 collective-permute-start.1
  24.2 0.0 collective-permute-start
  24.2 0.8 %shard_map.51.center_ref = f32[8,16,128]{2,1,0:T(8,128)S(1)} custom-call(f32[8,8,128]{2,1,0:T(8,128)S(1)} %all_to_all.15.field_ref.rhs_ref, bf16[8,2,9,128,128]{4,3,2,1,0:T(8,128)(2,1)S(1)} %get-tuple-element.7.links_ref), custom_call_target="tpu_custom_call" | custom-call | flops 41943040 | bytes 3000000 | tf_op jit(solution)/shard_map/pallas_call | solution.py:23
  25.0 0.0 collective-permute-done.3.d_ref
  25.0 0.8 %collective-permute-done.2.c_ref = f32[8,8,128]{2,1,0:T(8,128)S(1)} collective-permute-done((f32[8,8,128]{2,1,0:T(8,128)S(1)}, f32[8,8,128]{2,1,0:T(8,128)S(1)}, u32[]{:S(2)}, u32[]{:S(2)}) %collective-permute-start.2) | collective-permute-done | bytes 32800 | tf_op jit(solution)/shard_map/ppermute | solution.py:306
  25.8 1.1 %collective-permute-done.1.b_ref = f32[8,8,128]{2,1,0:T(8,128)S(1)} collective-permute-done((f32[8,8,128]{2,1,0:T(8,128)S(1)}, f32[8,8,128]{2,1,0:T(8,128)S(1)}, u32[]{:S(2)}, u32[]{:S(2)}) %collective-permute-start.1) | collective-permute-done | bytes 32800 | tf_op jit(solution)/shard_map/ppermute | solution.py:306
  27.0 0.0 collective-permute-done.a_ref
  27.0 0.7 %shard_map.52 = (f32[8,8,128]{2,1,0:T(8,128)S(1)}, f32[8,8,128]{2,1,0:T(8,128)S(1)}) custom-call(f32[8,16,128]{2,1,0:T(8,128)S(1)} %shard_map.51.center_ref, f32[8,8,128]{2,1,0:T(8,128)S(1)} %all_to_all.15.field_ref.rhs_ref, f32[8,8,128]{2,1,0:T(8,128)S(1)} %collective-permute-done.a_ref, f32[8,8,128]{2,1,0:T(8,128)S(1)} %collective-permute-done.1.b_ref, ...), custom_call_target="tpu_custom_call" | custom-call | flops 33554432 | bytes 2000000 | tf_op jit(solution)/shard_map/pallas_call | solution.py:23
  27.6 1.9 %collective-permute-start.7 = (f32[8,8,128]{2,1,0:T(8,128)S(1)}, f32[8,8,128]{2,1,0:T(8,128)S(1)}, u32[]{:S(2)}, u32[]{:S(2)}) collective-permute-start(f32[8,8,128]{2,1,0:T(8,128)S(1)} %get-tuple-element.8.field_ref.image_ref), channel_id=1, source_target_pairs={{1,2},{3,4},{5,6},{7,64},{65,66},{67,68},{69,70},{71,128},{129,130... | collective-permute-start | bytes 98312 | tf_op jit(solution)/shard_map/ppermute | solution.py:306
  29.5 1.7 %collective-permute-start.6 = (f32[8,8,128]{2,1,0:T(8,128)S(1)}, f32[8,8,128]{2,1,0:T(8,128)S(1)}, u32[]{:S(2)}, u32[]{:S(2)}) collective-permute-start(f32[8,8,128]{2,1,0:T(8,128)S(1)} %get-tuple-element.8.field_ref.image_ref), channel_id=1, source_target_pairs={{8,16},{24,32},{40,48},{56,0},{16,8},{32,24},{48,40},{0,56},{9,17}... | collective-permute-start | bytes 98312 | tf_op jit(solution)/shard_map/ppermute | solution.py:306
  31.2 0.7 %collective-permute-start.5 = (f32[8,8,128]{2,1,0:T(8,128)S(1)}, f32[8,8,128]{2,1,0:T(8,128)S(1)}, u32[]{:S(2)}, u32[]{:S(2)}) collective-permute-start(f32[8,8,128]{2,1,0:T(8,128)S(1)} %get-tuple-element.8.field_ref.image_ref), channel_id=1, source_target_pairs={{0,8},{16,24},{32,40},{48,56},{8,0},{24,16},{40,32},{56,48},{1,9},... | collective-permute-start | bytes 98312 | tf_op jit(solution)/shard_map/ppermute | solution.py:306
  32.0 0.0 collective-permute-start.4
  32.0 0.8 %shard_map.53.center_ref = f32[8,16,128]{2,1,0:T(8,128)S(1)} custom-call(f32[8,8,128]{2,1,0:T(8,128)S(1)} %get-tuple-element.8.field_ref.image_ref, bf16[8,2,9,128,128]{4,3,2,1,0:T(8,128)(2,1)S(1)} %get-tuple-element.7.links_ref), custom_call_target="tpu_custom_call" | custom-call | flops 41943040 | bytes 3000000 | tf_op jit(solution)/shard_map/pallas_call | solution.py:23
  32.7 0.4 collective-permute-done.7.d_ref
  33.2 0.3 collective-permute-done.6.c_ref
  33.5 0.8 %collective-permute-done.5.b_ref = f32[8,8,128]{2,1,0:T(8,128)S(1)} collective-permute-done((f32[8,8,128]{2,1,0:T(8,128)S(1)}, f32[8,8,128]{2,1,0:T(8,128)S(1)}, u32[]{:S(2)}, u32[]{:S(2)}) %collective-permute-start.5) | collective-permute-done | bytes 32800 | tf_op jit(solution)/shard_map/ppermute | solution.py:306
  34.3 0.7 %collective-permute-done.4.a_ref = f32[8,8,128]{2,1,0:T(8,128)S(1)} collective-permute-done((f32[8,8,128]{2,1,0:T(8,128)S(1)}, f32[8,8,128]{2,1,0:T(8,128)S(1)}, u32[]{:S(2)}, u32[]{:S(2)}) %collective-permute-start.4) | collective-permute-done | bytes 32800 | tf_op jit(solution)/shard_map/ppermute | solution.py:306
  35.0 0.8 %shard_map.54 = f32[8,32,128]{2,1,0:T(8,128)S(1)} custom-call(f32[8,16,128]{2,1,0:T(8,128)S(1)} %shard_map.53.center_ref, f32[8,8,128]{2,1,0:T(8,128)S(1)} %get-tuple-element.8.field_ref.image_ref, f32[8,8,128]{2,1,0:T(8,128)S(1)} %collective-permute-done.4.a_ref, f32[8,8,128]{2,1,0:T(8,128)S(1)} %collective-permute-done.5.b_ref, ...), custom_call_target="tpu_custom_call" | custom-call | flops 33554432 | bytes 2000000 | tf_op jit(solution)/shard_map/pallas_call | solution.py:23
  35.8 7.5 %all_to_all.16.packed_ref = f32[8,32,128]{2,1,0:T(8,128)S(1)} all-to-all(f32[8,32,128]{2,1,0:T(8,128)S(1)} %shard_map.54), channel_id=1, replica_groups={{4,5,6,7,0,1,2,3},{12,13,14,15,8,9,10,11},{20,21,22,23,16,17,18,19},{28..., dimensions={0} | all-to-all | bytes 262144 | tf_op jit(solution)/shard_map/all_to_all | solution.py:325
  43.3 0.6 %shard_map.55 = f32[32,1,128]{2,1,0:T(1,128)} custom-call(f32[8,32,128]{2,1,0:T(8,128)S(1)} %all_to_all.16.packed_ref), custom_call_target="tpu_custom_call" | custom-call | flops 10000 | bytes 50000 | tf_op jit(solution)/shard_map/pallas_call | solution.py:23
  43.9 11.5 %all-to-all-start.2 = ((f32[32,1,128]{2,1,0:T(1,128)}), f32[32,1,128]{2,1,0:T(1,128)S(1)}, u32[]{:S(2)}, u32[]{:S(2)}) async-start(f32[32,1,128]{2,1,0:T(1,128)} %shard_map.55), calls=%async_computation.2 | async-start | bytes 32768 | tf_op jit(solution)/shard_map/all_to_all | solution.py:325
  55.4 3.3 %shard_map.56.basis_ref = f32[8,64,1536]{2,1,0:T(8,128)S(1)} custom-call(f32[8,32,128]{2,1,0:T(8,128)S(1)} %all_to_all.16.packed_ref, f32[8,8,128]{2,1,0:T(8,128)S(1)} %get-tuple-element.6.rhs_ref, bf16[8,1,1,2,2,2,32,1536]{7,6,5,4,3,2,1,0:T(8,128)(2,1)} %vectors_hbm.3), custom_call_target="tpu_custom_call" | custom-call | flops 805306368 | bytes 10000000 | tf_op jit(solution)/shard_map/pallas_call | solution.py:23
  58.6 0.5 all-to-all-done.2.sums_ref
  59.1 1.2 %shard_map.57 = (bf16[4,8,1,1,2,2,2,1536]{7,6,5,4,3,2,1,0:T(2,128)(2,1)}, f32[4,8,1,1,2,128]{5,4,3,2,1,0:T(2,128)}) custom-call(f32[32,1,128]{2,1,0:T(1,128)S(1)} %all-to-all-done.2.sums_ref, f32[8,32,128]{2,1,0:T(8,128)S(1)} %all_to_all.16.packed_ref, f32[8,8,128]{2,1,0:T(8,128)S(1)} %get-tuple-element.6.rhs_ref, f32[8,64,1536]{2,1,0:T(8,128)S(1)} %shard_map.56.basis_ref), custom_call_target="tpu_custom_call" | custom-call | flops 2000000 | bytes 4000000 | tf_op jit(solution)/shard_map/pallas_call | solution.py:23
Async XLA Ops:
  14.6 10.4 %collective-permute-start.3 = (f32[8,8,128]{2,1,0:T(8,128)S(1)}, f32[8,8,128]{2,1,0:T(8,128)S(1)}, u32[]{:S(2)}, u32[]{:S(2)}) collective-permute-start(f32[8,8,128]{2,1,0:T(8,128)S(1)} %all_to_all.15.field_ref.rhs_ref), channel_id=1, source_target_pairs={{1,2},{3,4},{5,6},{7,64},{65,66},{67,68},{69,70},{71,128},{129,130... | collective-permute-start | bytes 98312 | tf_op jit(solution)/shard_map/ppermute | solution.py:306
  18.6 7.2 %collective-permute-start.2 = (f32[8,8,128]{2,1,0:T(8,128)S(1)}, f32[8,8,128]{2,1,0:T(8,128)S(1)}, u32[]{:S(2)}, u32[]{:S(2)}) collective-permute-start(f32[8,8,128]{2,1,0:T(8,128)S(1)} %all_to_all.15.field_ref.rhs_ref), channel_id=1, source_target_pairs={{8,16},{24,32},{40,48},{56,0},{16,8},{32,24},{48,40},{0,56},{9,17}... | collective-permute-start | bytes 98312 | tf_op jit(solution)/shard_map/ppermute | solution.py:306
  24.2 2.8 %collective-permute-start.1 = (f32[8,8,128]{2,1,0:T(8,128)S(1)}, f32[8,8,128]{2,1,0:T(8,128)S(1)}, u32[]{:S(2)}, u32[]{:S(2)}) collective-permute-start(f32[8,8,128]{2,1,0:T(8,128)S(1)} %all_to_all.15.field_ref.rhs_ref), channel_id=1, source_target_pairs={{0,8},{16,24},{32,40},{48,56},{8,0},{24,16},{40,32},{56,48},{1,9},... | collective-permute-start | bytes 98312 | tf_op jit(solution)/shard_map/ppermute | solution.py:306
  24.2 2.8 %collective-permute-start = (f32[8,8,128]{2,1,0:T(8,128)S(1)}, f32[8,8,128]{2,1,0:T(8,128)S(1)}, u32[]{:S(2)}, u32[]{:S(2)}) collective-permute-start(f32[8,8,128]{2,1,0:T(8,128)S(1)} %all_to_all.15.field_ref.rhs_ref), channel_id=1, source_target_pairs={{0,1},{2,3},{4,5},{6,7},{64,65},{66,67},{68,69},{70,71},{128,129},... | collective-permute-start | bytes 98312 | tf_op jit(solution)/shard_map/ppermute | solution.py:306
  27.6 5.5 %collective-permute-start.7 = (f32[8,8,128]{2,1,0:T(8,128)S(1)}, f32[8,8,128]{2,1,0:T(8,128)S(1)}, u32[]{:S(2)}, u32[]{:S(2)}) collective-permute-start(f32[8,8,128]{2,1,0:T(8,128)S(1)} %get-tuple-element.8.field_ref.image_ref), channel_id=1, source_target_pairs={{1,2},{3,4},{5,6},{7,64},{65,66},{67,68},{69,70},{71,128},{129,130... | collective-permute-start | bytes 98312 | tf_op jit(solution)/shard_map/ppermute | solution.py:306
  29.5 4.0 %collective-permute-start.6 = (f32[8,8,128]{2,1,0:T(8,128)S(1)}, f32[8,8,128]{2,1,0:T(8,128)S(1)}, u32[]{:S(2)}, u32[]{:S(2)}) collective-permute-start(f32[8,8,128]{2,1,0:T(8,128)S(1)} %get-tuple-element.8.field_ref.image_ref), channel_id=1, source_target_pairs={{8,16},{24,32},{40,48},{56,0},{16,8},{32,24},{48,40},{0,56},{9,17}... | collective-permute-start | bytes 98312 | tf_op jit(solution)/shard_map/ppermute | solution.py:306
  31.2 3.1 %collective-permute-start.5 = (f32[8,8,128]{2,1,0:T(8,128)S(1)}, f32[8,8,128]{2,1,0:T(8,128)S(1)}, u32[]{:S(2)}, u32[]{:S(2)}) collective-permute-start(f32[8,8,128]{2,1,0:T(8,128)S(1)} %get-tuple-element.8.field_ref.image_ref), channel_id=1, source_target_pairs={{0,8},{16,24},{32,40},{48,56},{8,0},{24,16},{40,32},{56,48},{1,9},... | collective-permute-start | bytes 98312 | tf_op jit(solution)/shard_map/ppermute | solution.py:306
  32.0 3.1 %collective-permute-start.4 = (f32[8,8,128]{2,1,0:T(8,128)S(1)}, f32[8,8,128]{2,1,0:T(8,128)S(1)}, u32[]{:S(2)}, u32[]{:S(2)}) collective-permute-start(f32[8,8,128]{2,1,0:T(8,128)S(1)} %get-tuple-element.8.field_ref.image_ref), channel_id=1, source_target_pairs={{0,1},{2,3},{4,5},{6,7},{64,65},{66,67},{68,69},{70,71},{128,129},... | collective-permute-start | bytes 98312 | tf_op jit(solution)/shard_map/ppermute | solution.py:306
  43.9 15.2 %all-to-all-start.2 = ((f32[32,1,128]{2,1,0:T(1,128)}), f32[32,1,128]{2,1,0:T(1,128)S(1)}, u32[]{:S(2)}, u32[]{:S(2)}) async-start(f32[32,1,128]{2,1,0:T(1,128)} %shard_map.55), calls=%async_computation.2 | async-start | bytes 32768 | tf_op jit(solution)/shard_map/all_to_all | solution.py:325

commit v5 on v4

--- a/solution.py
+++ b/solution.py
@@ -98,7 +98,7 @@
         copies[number].wait()
         for time in group:
             product = dot_nt(rows[time], vectors[time].reshape(256, -1))
-            full[time, 0], full[time, 1] = product[:, :DOF], product[:, DOF:]
+            full[time, 0, 0:32], full[time, 1, 0:32] = product[:, :DOF], product[:, DOF:]
         if number == 0:
             gather(groups[1])
         else:
@@ -348,7 +348,7 @@
             local_vectors,
             pltpu.VMEM(fine_source.shape, BF16),
             pltpu.VMEM((times, 32, length), BF16),
-            pltpu.VMEM((times, 2, 32, DOF), F32),
+            pltpu.VMEM((times, 2, 40, DOF), F32),
             pltpu.SemaphoreType.DMA,
             pltpu.SemaphoreType.DMA((2,)),
             pltpu.SemaphoreType.DMA,

time: 60.6 us -> 60.6 us (level)
  no operation moved by 1% of the time
where the time goes in v5:
time: 60.6 us; the launch traced here: 60.4 us
  starting transfers between devices  25.4 us (42%)
  blocking collectives  16.8 us (28%)
  Pallas kernels  12.8 us (21%)
  waiting for transfers between devices  4.74 us (8%)
  between operations  0.67 us (1%)
    all_to_all x2, blocking collectives, exchange(): lax.all_to_all(array, axis, split_axis=0, concat_axis=0, tiled=True, axis...  16.8 us
    ppermute x8, starting transfers between devices, neighbours(): found.append(lax.ppermute(field, axis, pairs + [(j, i) for i, j in pairs]))  13.9 us
    pallas_call x8, Pallas kernels, call(): pl.pallas_call(kernel, out_shape=out_shape, in_specs=inputs if isinstance...  12.8 us
    all_to_all x1, starting transfers between devices, exchange(): lax.all_to_all(array, axis, split_axis=0, concat_axis=0, tiled=True, axis...  11.5 us
    ppermute x8, waiting for transfers between devices, neighbours(): found.append(lax.ppermute(field, axis, pairs + [(j, i) for i, j in pairs]))  4.26 us
  transfers between devices with their start and end apart: 9, of which 7 were waited for; matrix products, arithmetic and copies ran while one was open for 0% of the time, Pallas kernels for 8%

profile of v5, /device:TPU:1, one launch (start us, length us, event | category | flops | bytes accessed | tf_op | source)
XLA Modules:
  0.0 60.4 jit_solution(10154986403610760556)
XLA Ops:
  0.6 4.6 %shard_map.50 = (f32[8,8,128]{2,1,0:T(8,128)S(1)}, bf16[8,2,9,128,128]{4,3,2,1,0:T(8,128)(2,1)S(1)}) custom-call(bf16[4,8,1,1,2,2,2,1536]{7,6,5,4,3,2,1,0:T(2,128)(2,1)} %source_hbm.1, bf16[8,1,1,2,2,2,32,1536]{7,6,5,4,3,2,1,0:T(8,128)(2,1)} %vectors_hbm.3, bf16[1,1,8,2,9,128,128]{6,5,4,3,2,1,0:T(8,128)(2,1)} %links_hbm.1), custom_call_target="tpu_custom_call" | custom-call | flops 201326592 | bytes 12000000 | tf_op jit(solution)/shard_map/pallas_call | solution.py:23
  5.3 9.3 %all_to_all.15.field_ref.rhs_ref = f32[8,8,128]{2,1,0:T(8,128)S(1)} all-to-all(f32[8,8,128]{2,1,0:T(8,128)S(1)} %get-tuple-element.6.rhs_ref), channel_id=1, replica_groups={{4,5,6,7,0,1,2,3},{12,13,14,15,8,9,10,11},{20,21,22,23,16,17,18,19},{28..., dimensions={0} | all-to-all | bytes 65536 | tf_op jit(solution)/shard_map/all_to_all | solution.py:325
  14.6 4.0 %collective-permute-start.3 = (f32[8,8,128]{2,1,0:T(8,128)S(1)}, f32[8,8,128]{2,1,0:T(8,128)S(1)}, u32[]{:S(2)}, u32[]{:S(2)}) collective-permute-start(f32[8,8,128]{2,1,0:T(8,128)S(1)} %all_to_all.15.field_ref.rhs_ref), channel_id=1, source_target_pairs={{1,2},{3,4},{5,6},{7,64},{65,66},{67,68},{69,70},{71,128},{129,130... | collective-permute-start | bytes 98312 | tf_op jit(solution)/shard_map/ppermute | solution.py:306
  18.6 5.5 %collective-permute-start.2 = (f32[8,8,128]{2,1,0:T(8,128)S(1)}, f32[8,8,128]{2,1,0:T(8,128)S(1)}, u32[]{:S(2)}, u32[]{:S(2)}) collective-permute-start(f32[8,8,128]{2,1,0:T(8,128)S(1)} %all_to_all.15.field_ref.rhs_ref), channel_id=1, source_target_pairs={{8,16},{24,32},{40,48},{56,0},{16,8},{32,24},{48,40},{0,56},{9,17}... | collective-permute-start | bytes 98312 | tf_op jit(solution)/shard_map/ppermute | solution.py:306
  24.2 0.0 collective-permute-start.1
  24.2 0.0 collective-permute-start
  24.2 0.8 %shard_map.51.center_ref = f32[8,16,128]{2,1,0:T(8,128)S(1)} custom-call(f32[8,8,128]{2,1,0:T(8,128)S(1)} %all_to_all.15.field_ref.rhs_ref, bf16[8,2,9,128,128]{4,3,2,1,0:T(8,128)(2,1)S(1)} %get-tuple-element.7.links_ref), custom_call_target="tpu_custom_call" | custom-call | flops 41943040 | bytes 3000000 | tf_op jit(solution)/shard_map/pallas_call | solution.py:23
  25.0 0.0 collective-permute-done.3.d_ref
  25.0 1.1 %collective-permute-done.2.c_ref = f32[8,8,128]{2,1,0:T(8,128)S(1)} collective-permute-done((f32[8,8,128]{2,1,0:T(8,128)S(1)}, f32[8,8,128]{2,1,0:T(8,128)S(1)}, u32[]{:S(2)}, u32[]{:S(2)}) %collective-permute-start.2) | collective-permute-done | bytes 32800 | tf_op jit(solution)/shard_map/ppermute | solution.py:306
  26.1 0.8 %collective-permute-done.1.b_ref = f32[8,8,128]{2,1,0:T(8,128)S(1)} collective-permute-done((f32[8,8,128]{2,1,0:T(8,128)S(1)}, f32[8,8,128]{2,1,0:T(8,128)S(1)}, u32[]{:S(2)}, u32[]{:S(2)}) %collective-permute-start.1) | collective-permute-done | bytes 32800 | tf_op jit(solution)/shard_map/ppermute | solution.py:306
  27.0 0.0 collective-permute-done.a_ref
  27.0 0.7 %shard_map.52 = (f32[8,8,128]{2,1,0:T(8,128)S(1)}, f32[8,8,128]{2,1,0:T(8,128)S(1)}) custom-call(f32[8,16,128]{2,1,0:T(8,128)S(1)} %shard_map.51.center_ref, f32[8,8,128]{2,1,0:T(8,128)S(1)} %all_to_all.15.field_ref.rhs_ref, f32[8,8,128]{2,1,0:T(8,128)S(1)} %collective-permute-done.a_ref, f32[8,8,128]{2,1,0:T(8,128)S(1)} %collective-permute-done.1.b_ref, ...), custom_call_target="tpu_custom_call" | custom-call | flops 33554432 | bytes 2000000 | tf_op jit(solution)/shard_map/pallas_call | solution.py:23
  27.6 1.9 %collective-permute-start.7 = (f32[8,8,128]{2,1,0:T(8,128)S(1)}, f32[8,8,128]{2,1,0:T(8,128)S(1)}, u32[]{:S(2)}, u32[]{:S(2)}) collective-permute-start(f32[8,8,128]{2,1,0:T(8,128)S(1)} %get-tuple-element.8.field_ref.image_ref), channel_id=1, source_target_pairs={{1,2},{3,4},{5,6},{7,64},{65,66},{67,68},{69,70},{71,128},{129,130... | collective-permute-start | bytes 98312 | tf_op jit(solution)/shard_map/ppermute | solution.py:306
  29.5 1.7 %collective-permute-start.6 = (f32[8,8,128]{2,1,0:T(8,128)S(1)}, f32[8,8,128]{2,1,0:T(8,128)S(1)}, u32[]{:S(2)}, u32[]{:S(2)}) collective-permute-start(f32[8,8,128]{2,1,0:T(8,128)S(1)} %get-tuple-element.8.field_ref.image_ref), channel_id=1, source_target_pairs={{8,16},{24,32},{40,48},{56,0},{16,8},{32,24},{48,40},{0,56},{9,17}... | collective-permute-start | bytes 98312 | tf_op jit(solution)/shard_map/ppermute | solution.py:306
  31.2 0.7 %collective-permute-start.5 = (f32[8,8,128]{2,1,0:T(8,128)S(1)}, f32[8,8,128]{2,1,0:T(8,128)S(1)}, u32[]{:S(2)}, u32[]{:S(2)}) collective-permute-start(f32[8,8,128]{2,1,0:T(8,128)S(1)} %get-tuple-element.8.field_ref.image_ref), channel_id=1, source_target_pairs={{0,8},{16,24},{32,40},{48,56},{8,0},{24,16},{40,32},{56,48},{1,9},... | collective-permute-start | bytes 98312 | tf_op jit(solution)/shard_map/ppermute | solution.py:306
  32.0 0.0 collective-permute-start.4
  32.0 0.8 %shard_map.53.center_ref = f32[8,16,128]{2,1,0:T(8,128)S(1)} custom-call(f32[8,8,128]{2,1,0:T(8,128)S(1)} %get-tuple-element.8.field_ref.image_ref, bf16[8,2,9,128,128]{4,3,2,1,0:T(8,128)(2,1)S(1)} %get-tuple-element.7.links_ref), custom_call_target="tpu_custom_call" | custom-call | flops 41943040 | bytes 3000000 | tf_op jit(solution)/shard_map/pallas_call | solution.py:23
  32.7 0.4 collective-permute-done.7.d_ref
  33.2 0.3 collective-permute-done.6.c_ref
  33.5 0.8 %collective-permute-done.5.b_ref = f32[8,8,128]{2,1,0:T(8,128)S(1)} collective-permute-done((f32[8,8,128]{2,1,0:T(8,128)S(1)}, f32[8,8,128]{2,1,0:T(8,128)S(1)}, u32[]{:S(2)}, u32[]{:S(2)}) %collective-permute-start.5) | collective-permute-done | bytes 32800 | tf_op jit(solution)/shard_map/ppermute | solution.py:306
  34.3 0.7 %collective-permute-done.4.a_ref = f32[8,8,128]{2,1,0:T(8,128)S(1)} collective-permute-done((f32[8,8,128]{2,1,0:T(8,128)S(1)}, f32[8,8,128]{2,1,0:T(8,128)S(1)}, u32[]{:S(2)}, u32[]{:S(2)}) %collective-permute-start.4) | collective-permute-done | bytes 32800 | tf_op jit(solution)/shard_map/ppermute | solution.py:306
  35.0 0.8 %shard_map.54 = f32[8,32,128]{2,1,0:T(8,128)S(1)} custom-call(f32[8,16,128]{2,1,0:T(8,128)S(1)} %shard_map.53.center_ref, f32[8,8,128]{2,1,0:T(8,128)S(1)} %get-tuple-element.8.field_ref.image_ref, f32[8,8,128]{2,1,0:T(8,128)S(1)} %collective-permute-done.4.a_ref, f32[8,8,128]{2,1,0:T(8,128)S(1)} %collective-permute-done.5.b_ref, ...), custom_call_target="tpu_custom_call" | custom-call | flops 33554432 | bytes 2000000 | tf_op jit(solution)/shard_map/pallas_call | solution.py:23
  35.8 7.5 %all_to_all.16.packed_ref = f32[8,32,128]{2,1,0:T(8,128)S(1)} all-to-all(f32[8,32,128]{2,1,0:T(8,128)S(1)} %shard_map.54), channel_id=1, replica_groups={{4,5,6,7,0,1,2,3},{12,13,14,15,8,9,10,11},{20,21,22,23,16,17,18,19},{28..., dimensions={0} | all-to-all | bytes 262144 | tf_op jit(solution)/shard_map/all_to_all | solution.py:325
  43.3 0.6 %shard_map.55 = f32[32,1,128]{2,1,0:T(1,128)} custom-call(f32[8,32,128]{2,1,0:T(8,128)S(1)} %all_to_all.16.packed_ref), custom_call_target="tpu_custom_call" | custom-call | flops 10000 | bytes 50000 | tf_op jit(solution)/shard_map/pallas_call | solution.py:23
  43.9 11.5 %all-to-all-start.2 = ((f32[32,1,128]{2,1,0:T(1,128)}), f32[32,1,128]{2,1,0:T(1,128)S(1)}, u32[]{:S(2)}, u32[]{:S(2)}) async-start(f32[32,1,128]{2,1,0:T(1,128)} %shard_map.55), calls=%async_computation.2 | async-start | bytes 32768 | tf_op jit(solution)/shard_map/all_to_all | solution.py:325
  55.4 3.3 %shard_map.56.basis_ref = f32[8,64,1536]{2,1,0:T(8,128)S(1)} custom-call(f32[8,32,128]{2,1,0:T(8,128)S(1)} %all_to_all.16.packed_ref, f32[8,8,128]{2,1,0:T(8,128)S(1)} %get-tuple-element.6.rhs_ref, bf16[8,1,1,2,2,2,32,1536]{7,6,5,4,3,2,1,0:T(8,128)(2,1)} %vectors_hbm.3), custom_call_target="tpu_custom_call" | custom-call | flops 805306368 | bytes 10000000 | tf_op jit(solution)/shard_map/pallas_call | solution.py:23
  58.6 0.5 all-to-all-done.2.sums_ref
  59.1 1.2 %shard_map.57 = (bf16[4,8,1,1,2,2,2,1536]{7,6,5,4,3,2,1,0:T(2,128)(2,1)}, f32[4,8,1,1,2,128]{5,4,3,2,1,0:T(2,128)}) custom-call(f32[32,1,128]{2,1,0:T(1,128)S(1)} %all-to-all-done.2.sums_ref, f32[8,32,128]{2,1,0:T(8,128)S(1)} %all_to_all.16.packed_ref, f32[8,8,128]{2,1,0:T(8,128)S(1)} %get-tuple-element.6.rhs_ref, f32[8,64,1536]{2,1,0:T(8,128)S(1)} %shard_map.56.basis_ref), custom_call_target="tpu_custom_call" | custom-call | flops 2000000 | bytes 4000000 | tf_op jit(solution)/shard_map/pallas_call | solution.py:23
Async XLA Ops:
  14.6 10.4 %collective-permute-start.3 = (f32[8,8,128]{2,1,0:T(8,128)S(1)}, f32[8,8,128]{2,1,0:T(8,128)S(1)}, u32[]{:S(2)}, u32[]{:S(2)}) collective-permute-start(f32[8,8,128]{2,1,0:T(8,128)S(1)} %all_to_all.15.field_ref.rhs_ref), channel_id=1, source_target_pairs={{1,2},{3,4},{5,6},{7,64},{65,66},{67,68},{69,70},{71,128},{129,130... | collective-permute-start | bytes 98312 | tf_op jit(solution)/shard_map/ppermute | solution.py:306
  18.6 7.5 %collective-permute-start.2 = (f32[8,8,128]{2,1,0:T(8,128)S(1)}, f32[8,8,128]{2,1,0:T(8,128)S(1)}, u32[]{:S(2)}, u32[]{:S(2)}) collective-permute-start(f32[8,8,128]{2,1,0:T(8,128)S(1)} %all_to_all.15.field_ref.rhs_ref), channel_id=1, source_target_pairs={{8,16},{24,32},{40,48},{56,0},{16,8},{32,24},{48,40},{0,56},{9,17}... | collective-permute-start | bytes 98312 | tf_op jit(solution)/shard_map/ppermute | solution.py:306
  24.2 2.8 %collective-permute-start.1 = (f32[8,8,128]{2,1,0:T(8,128)S(1)}, f32[8,8,128]{2,1,0:T(8,128)S(1)}, u32[]{:S(2)}, u32[]{:S(2)}) collective-permute-start(f32[8,8,128]{2,1,0:T(8,128)S(1)} %all_to_all.15.field_ref.rhs_ref), channel_id=1, source_target_pairs={{0,8},{16,24},{32,40},{48,56},{8,0},{24,16},{40,32},{56,48},{1,9},... | collective-permute-start | bytes 98312 | tf_op jit(solution)/shard_map/ppermute | solution.py:306
  24.2 2.8 %collective-permute-start = (f32[8,8,128]{2,1,0:T(8,128)S(1)}, f32[8,8,128]{2,1,0:T(8,128)S(1)}, u32[]{:S(2)}, u32[]{:S(2)}) collective-permute-start(f32[8,8,128]{2,1,0:T(8,128)S(1)} %all_to_all.15.field_ref.rhs_ref), channel_id=1, source_target_pairs={{0,1},{2,3},{4,5},{6,7},{64,65},{66,67},{68,69},{70,71},{128,129},... | collective-permute-start | bytes 98312 | tf_op jit(solution)/shard_map/ppermute | solution.py:306
  27.6 5.5 %collective-permute-start.7 = (f32[8,8,128]{2,1,0:T(8,128)S(1)}, f32[8,8,128]{2,1,0:T(8,128)S(1)}, u32[]{:S(2)}, u32[]{:S(2)}) collective-permute-start(f32[8,8,128]{2,1,0:T(8,128)S(1)} %get-tuple-element.8.field_ref.image_ref), channel_id=1, source_target_pairs={{1,2},{3,4},{5,6},{7,64},{65,66},{67,68},{69,70},{71,128},{129,130... | collective-permute-start | bytes 98312 | tf_op jit(solution)/shard_map/ppermute | solution.py:306
  29.5 4.0 %collective-permute-start.6 = (f32[8,8,128]{2,1,0:T(8,128)S(1)}, f32[8,8,128]{2,1,0:T(8,128)S(1)}, u32[]{:S(2)}, u32[]{:S(2)}) collective-permute-start(f32[8,8,128]{2,1,0:T(8,128)S(1)} %get-tuple-element.8.field_ref.image_ref), channel_id=1, source_target_pairs={{8,16},{24,32},{40,48},{56,0},{16,8},{32,24},{48,40},{0,56},{9,17}... | collective-permute-start | bytes 98312 | tf_op jit(solution)/shard_map/ppermute | solution.py:306
  31.2 3.1 %collective-permute-start.5 = (f32[8,8,128]{2,1,0:T(8,128)S(1)}, f32[8,8,128]{2,1,0:T(8,128)S(1)}, u32[]{:S(2)}, u32[]{:S(2)}) collective-permute-start(f32[8,8,128]{2,1,0:T(8,128)S(1)} %get-tuple-element.8.field_ref.image_ref), channel_id=1, source_target_pairs={{0,8},{16,24},{32,40},{48,56},{8,0},{24,16},{40,32},{56,48},{1,9},... | collective-permute-start | bytes 98312 | tf_op jit(solution)/shard_map/ppermute | solution.py:306
  32.0 3.1 %collective-permute-start.4 = (f32[8,8,128]{2,1,0:T(8,128)S(1)}, f32[8,8,128]{2,1,0:T(8,128)S(1)}, u32[]{:S(2)}, u32[]{:S(2)}) collective-permute-start(f32[8,8,128]{2,1,0:T(8,128)S(1)} %get-tuple-element.8.field_ref.image_ref), channel_id=1, source_target_pairs={{0,1},{2,3},{4,5},{6,7},{64,65},{66,67},{68,69},{70,71},{128,129},... | collective-permute-start | bytes 98312 | tf_op jit(solution)/shard_map/ppermute | solution.py:306
  43.9 15.2 %all-to-all-start.2 = ((f32[32,1,128]{2,1,0:T(1,128)}), f32[32,1,128]{2,1,0:T(1,128)S(1)}, u32[]{:S(2)}, u32[]{:S(2)}) async-start(f32[32,1,128]{2,1,0:T(1,128)} %shard_map.55), calls=%async_computation.2 | async-start | bytes 32768 | tf_op jit(solution)/shard_map/all_to_all | solution.py:325

commit v6 on v5

--- a/solution.py
+++ b/solution.py
@@ -268,9 +268,9 @@
 ):
     times = packed_ref.shape[0]
     total = jnp.sum(sums_ref[...], axis=0)
-    alpha_zero, alpha_one, beta, kappa = coefficients(total, (index((32, DOF), 0) // 2) % RHS)
-    keep_rhs = alpha_zero + alpha_one * (1.0 - beta)
-    keep_image = -alpha_one * alpha_zero
+    alpha_zero, alpha_one, beta, kappa = coefficients(total, (index((ROWS, DOF), 0) // 2) % RHS)
+    keep_rhs = jnp.concatenate([alpha_zero + alpha_one * (1.0 - beta)] * 4, axis=0)
+    keep_image = jnp.concatenate([-alpha_one * alpha_zero] * 4, axis=0)
     copies = []
     for time in range(times):
         fields = (keep_rhs * basis_ref[time, 0:32] + keep_image * basis_ref[time, 32:64]).astype(BF16)

time: 60.6 us -> 60.6 us (level)
  no operation moved by 1% of the time
where the time goes in v6:
time: 60.6 us; the launch traced here: 60.4 us
  starting transfers between devices  25.4 us (42%)
  blocking collectives  16.8 us (28%)
  Pallas kernels  12.8 us (21%)
  waiting for transfers between devices  4.74 us (8%)
  between operations  0.67 us (1%)
    all_to_all x2, blocking collectives, exchange(): lax.all_to_all(array, axis, split_axis=0, concat_axis=0, tiled=True, axis...  16.8 us
    ppermute x8, starting transfers between devices, neighbours(): found.append(lax.ppermute(field, axis, pairs + [(j, i) for i, j in pairs]))  13.9 us
    pallas_call x8, Pallas kernels, call(): pl.pallas_call(kernel, out_shape=out_shape, in_specs=inputs if isinstance...  12.8 us
    all_to_all x1, starting transfers between devices, exchange(): lax.all_to_all(array, axis, split_axis=0, concat_axis=0, tiled=True, axis...  11.5 us
    ppermute x8, waiting for transfers between devices, neighbours(): found.append(lax.ppermute(field, axis, pairs + [(j, i) for i, j in pairs]))  4.26 us
  transfers between devices with their start and end apart: 9, of which 7 were waited for; matrix products, arithmetic and copies ran while one was open for 0% of the time, Pallas kernels for 8%

profile of v6, /device:TPU:1, one launch (start us, length us, event | category | flops | bytes accessed | tf_op | source)
XLA Modules:
  0.0 60.4 jit_solution(8222600462907553883)
XLA Ops:
  0.6 4.6 %shard_map.50 = (f32[8,8,128]{2,1,0:T(8,128)S(1)}, bf16[8,2,9,128,128]{4,3,2,1,0:T(8,128)(2,1)S(1)}) custom-call(bf16[4,8,1,1,2,2,2,1536]{7,6,5,4,3,2,1,0:T(2,128)(2,1)} %source_hbm.1, bf16[8,1,1,2,2,2,32,1536]{7,6,5,4,3,2,1,0:T(8,128)(2,1)} %vectors_hbm.3, bf16[1,1,8,2,9,128,128]{6,5,4,3,2,1,0:T(8,128)(2,1)} %links_hbm.1), custom_call_target="tpu_custom_call" | custom-call | flops 201326592 | bytes 12000000 | tf_op jit(solution)/shard_map/pallas_call | solution.py:23
  5.3 9.3 %all_to_all.15.field_ref.rhs_ref = f32[8,8,128]{2,1,0:T(8,128)S(1)} all-to-all(f32[8,8,128]{2,1,0:T(8,128)S(1)} %get-tuple-element.6.rhs_ref), channel_id=1, replica_groups={{4,5,6,7,0,1,2,3},{12,13,14,15,8,9,10,11},{20,21,22,23,16,17,18,19},{28..., dimensions={0} | all-to-all | bytes 65536 | tf_op jit(solution)/shard_map/all_to_all | solution.py:325
  14.6 4.0 %collective-permute-start.3 = (f32[8,8,128]{2,1,0:T(8,128)S(1)}, f32[8,8,128]{2,1,0:T(8,128)S(1)}, u32[]{:S(2)}, u32[]{:S(2)}) collective-permute-start(f32[8,8,128]{2,1,0:T(8,128)S(1)} %all_to_all.15.field_ref.rhs_ref), channel_id=1, source_target_pairs={{1,2},{3,4},{5,6},{7,64},{65,66},{67,68},{69,70},{71,128},{129,130... | collective-permute-start | bytes 98312 | tf_op jit(solution)/shard_map/ppermute | solution.py:306
  18.6 5.5 %collective-permute-start.2 = (f32[8,8,128]{2,1,0:T(8,128)S(1)}, f32[8,8,128]{2,1,0:T(8,128)S(1)}, u32[]{:S(2)}, u32[]{:S(2)}) collective-permute-start(f32[8,8,128]{2,1,0:T(8,128)S(1)} %all_to_all.15.field_ref.rhs_ref), channel_id=1, source_target_pairs={{8,16},{24,32},{40,48},{56,0},{16,8},{32,24},{48,40},{0,56},{9,17}... | collective-permute-start | bytes 98312 | tf_op jit(solution)/shard_map/ppermute | solution.py:306
  24.2 0.0 collective-permute-start.1
  24.2 0.0 collective-permute-start
  24.2 0.8 %shard_map.51.center_ref = f32[8,16,128]{2,1,0:T(8,128)S(1)} custom-call(f32[8,8,128]{2,1,0:T(8,128)S(1)} %all_to_all.15.field_ref.rhs_ref, bf16[8,2,9,128,128]{4,3,2,1,0:T(8,128)(2,1)S(1)} %get-tuple-element.7.links_ref), custom_call_target="tpu_custom_call" | custom-call | flops 41943040 | bytes 3000000 | tf_op jit(solution)/shard_map/pallas_call | solution.py:23
  25.0 0.0 collective-permute-done.3.d_ref
  25.0 1.1 %collective-permute-done.2.c_ref = f32[8,8,128]{2,1,0:T(8,128)S(1)} collective-permute-done((f32[8,8,128]{2,1,0:T(8,128)S(1)}, f32[8,8,128]{2,1,0:T(8,128)S(1)}, u32[]{:S(2)}, u32[]{:S(2)}) %collective-permute-start.2) | collective-permute-done | bytes 32800 | tf_op jit(solution)/shard_map/ppermute | solution.py:306
  26.1 0.8 %collective-permute-done.1.b_ref = f32[8,8,128]{2,1,0:T(8,128)S(1)} collective-permute-done((f32[8,8,128]{2,1,0:T(8,128)S(1)}, f32[8,8,128]{2,1,0:T(8,128)S(1)}, u32[]{:S(2)}, u32[]{:S(2)}) %collective-permute-start.1) | collective-permute-done | bytes 32800 | tf_op jit(solution)/shard_map/ppermute | solution.py:306
  27.0 0.0 collective-permute-done.a_ref
  27.0 0.7 %shard_map.52 = (f32[8,8,128]{2,1,0:T(8,128)S(1)}, f32[8,8,128]{2,1,0:T(8,128)S(1)}) custom-call(f32[8,16,128]{2,1,0:T(8,128)S(1)} %shard_map.51.center_ref, f32[8,8,128]{2,1,0:T(8,128)S(1)} %all_to_all.15.field_ref.rhs_ref, f32[8,8,128]{2,1,0:T(8,128)S(1)} %collective-permute-done.a_ref, f32[8,8,128]{2,1,0:T(8,128)S(1)} %collective-permute-done.1.b_ref, ...), custom_call_target="tpu_custom_call" | custom-call | flops 33554432 | bytes 2000000 | tf_op jit(solution)/shard_map/pallas_call | solution.py:23
  27.6 1.9 %collective-permute-start.7 = (f32[8,8,128]{2,1,0:T(8,128)S(1)}, f32[8,8,128]{2,1,0:T(8,128)S(1)}, u32[]{:S(2)}, u32[]{:S(2)}) collective-permute-start(f32[8,8,128]{2,1,0:T(8,128)S(1)} %get-tuple-element.8.field_ref.image_ref), channel_id=1, source_target_pairs={{1,2},{3,4},{5,6},{7,64},{65,66},{67,68},{69,70},{71,128},{129,130... | collective-permute-start | bytes 98312 | tf_op jit(solution)/shard_map/ppermute | solution.py:306
  29.5 1.7 %collective-permute-start.6 = (f32[8,8,128]{2,1,0:T(8,128)S(1)}, f32[8,8,128]{2,1,0:T(8,128)S(1)}, u32[]{:S(2)}, u32[]{:S(2)}) collective-permute-start(f32[8,8,128]{2,1,0:T(8,128)S(1)} %get-tuple-element.8.field_ref.image_ref), channel_id=1, source_target_pairs={{8,16},{24,32},{40,48},{56,0},{16,8},{32,24},{48,40},{0,56},{9,17}... | collective-permute-start | bytes 98312 | tf_op jit(solution)/shard_map/ppermute | solution.py:306
  31.2 0.7 %collective-permute-start.5 = (f32[8,8,128]{2,1,0:T(8,128)S(1)}, f32[8,8,128]{2,1,0:T(8,128)S(1)}, u32[]{:S(2)}, u32[]{:S(2)}) collective-permute-start(f32[8,8,128]{2,1,0:T(8,128)S(1)} %get-tuple-element.8.field_ref.image_ref), channel_id=1, source_target_pairs={{0,8},{16,24},{32,40},{48,56},{8,0},{24,16},{40,32},{56,48},{1,9},... | collective-permute-start | bytes 98312 | tf_op jit(solution)/shard_map/ppermute | solution.py:306
  32.0 0.0 collective-permute-start.4
  32.0 0.8 %shard_map.53.center_ref = f32[8,16,128]{2,1,0:T(8,128)S(1)} custom-call(f32[8,8,128]{2,1,0:T(8,128)S(1)} %get-tuple-element.8.field_ref.image_ref, bf16[8,2,9,128,128]{4,3,2,1,0:T(8,128)(2,1)S(1)} %get-tuple-element.7.links_ref), custom_call_target="tpu_custom_call" | custom-call | flops 41943040 | bytes 3000000 | tf_op jit(solution)/shard_map/pallas_call | solution.py:23
  32.7 0.4 collective-permute-done.7.d_ref
  33.2 0.3 collective-permute-done.6.c_ref
  33.5 0.8 %collective-permute-done.5.b_ref = f32[8,8,128]{2,1,0:T(8,128)S(1)} collective-permute-done((f32[8,8,128]{2,1,0:T(8,128)S(1)}, f32[8,8,128]{2,1,0:T(8,128)S(1)}, u32[]{:S(2)}, u32[]{:S(2)}) %collective-permute-start.5) | collective-permute-done | bytes 32800 | tf_op jit(solution)/shard_map/ppermute | solution.py:306
  34.3 0.7 %collective-permute-done.4.a_ref = f32[8,8,128]{2,1,0:T(8,128)S(1)} collective-permute-done((f32[8,8,128]{2,1,0:T(8,128)S(1)}, f32[8,8,128]{2,1,0:T(8,128)S(1)}, u32[]{:S(2)}, u32[]{:S(2)}) %collective-permute-start.4) | collective-permute-done | bytes 32800 | tf_op jit(solution)/shard_map/ppermute | solution.py:306
  35.0 0.8 %shard_map.54 = f32[8,32,128]{2,1,0:T(8,128)S(1)} custom-call(f32[8,16,128]{2,1,0:T(8,128)S(1)} %shard_map.53.center_ref, f32[8,8,128]{2,1,0:T(8,128)S(1)} %get-tuple-element.8.field_ref.image_ref, f32[8,8,128]{2,1,0:T(8,128)S(1)} %collective-permute-done.4.a_ref, f32[8,8,128]{2,1,0:T(8,128)S(1)} %collective-permute-done.5.b_ref, ...), custom_call_target="tpu_custom_call" | custom-call | flops 33554432 | bytes 2000000 | tf_op jit(solution)/shard_map/pallas_call | solution.py:23
  35.8 7.5 %all_to_all.16.packed_ref = f32[8,32,128]{2,1,0:T(8,128)S(1)} all-to-all(f32[8,32,128]{2,1,0:T(8,128)S(1)} %shard_map.54), channel_id=1, replica_groups={{4,5,6,7,0,1,2,3},{12,13,14,15,8,9,10,11},{20,21,22,23,16,17,18,19},{28..., dimensions={0} | all-to-all | bytes 262144 | tf_op jit(solution)/shard_map/all_to_all | solution.py:325
  43.3 0.6 %shard_map.55 = f32[32,1,128]{2,1,0:T(1,128)} custom-call(f32[8,32,128]{2,1,0:T(8,128)S(1)} %all_to_all.16.packed_ref), custom_call_target="tpu_custom_call" | custom-call | flops 10000 | bytes 50000 | tf_op jit(solution)/shard_map/pallas_call | solution.py:23
  43.9 11.5 %all-to-all-start.2 = ((f32[32,1,128]{2,1,0:T(1,128)}), f32[32,1,128]{2,1,0:T(1,128)S(1)}, u32[]{:S(2)}, u32[]{:S(2)}) async-start(f32[32,1,128]{2,1,0:T(1,128)} %shard_map.55), calls=%async_computation.2 | async-start | bytes 32768 | tf_op jit(solution)/shard_map/all_to_all | solution.py:325
  55.4 3.3 %shard_map.56.basis_ref = f32[8,64,1536]{2,1,0:T(8,128)S(1)} custom-call(f32[8,32,128]{2,1,0:T(8,128)S(1)} %all_to_all.16.packed_ref, f32[8,8,128]{2,1,0:T(8,128)S(1)} %get-tuple-element.6.rhs_ref, bf16[8,1,1,2,2,2,32,1536]{7,6,5,4,3,2,1,0:T(8,128)(2,1)} %vectors_hbm.3), custom_call_target="tpu_custom_call" | custom-call | flops 805306368 | bytes 10000000 | tf_op jit(solution)/shard_map/pallas_call | solution.py:23
  58.6 0.5 all-to-all-done.2.sums_ref
  59.1 1.3 %shard_map.57 = (bf16[4,8,1,1,2,2,2,1536]{7,6,5,4,3,2,1,0:T(2,128)(2,1)}, f32[4,8,1,1,2,128]{5,4,3,2,1,0:T(2,128)}) custom-call(f32[32,1,128]{2,1,0:T(1,128)S(1)} %all-to-all-done.2.sums_ref, f32[8,32,128]{2,1,0:T(8,128)S(1)} %all_to_all.16.packed_ref, f32[8,8,128]{2,1,0:T(8,128)S(1)} %get-tuple-element.6.rhs_ref, f32[8,64,1536]{2,1,0:T(8,128)S(1)} %shard_map.56.basis_ref), custom_call_target="tpu_custom_call" | custom-call | flops 2000000 | bytes 4000000 | tf_op jit(solution)/shard_map/pallas_call | solution.py:23
Async XLA Ops:
  14.6 10.4 %collective-permute-start.3 = (f32[8,8,128]{2,1,0:T(8,128)S(1)}, f32[8,8,128]{2,1,0:T(8,128)S(1)}, u32[]{:S(2)}, u32[]{:S(2)}) collective-permute-start(f32[8,8,128]{2,1,0:T(8,128)S(1)} %all_to_all.15.field_ref.rhs_ref), channel_id=1, source_target_pairs={{1,2},{3,4},{5,6},{7,64},{65,66},{67,68},{69,70},{71,128},{129,130... | collective-permute-start | bytes 98312 | tf_op jit(solution)/shard_map/ppermute | solution.py:306
  18.6 7.5 %collective-permute-start.2 = (f32[8,8,128]{2,1,0:T(8,128)S(1)}, f32[8,8,128]{2,1,0:T(8,128)S(1)}, u32[]{:S(2)}, u32[]{:S(2)}) collective-permute-start(f32[8,8,128]{2,1,0:T(8,128)S(1)} %all_to_all.15.field_ref.rhs_ref), channel_id=1, source_target_pairs={{8,16},{24,32},{40,48},{56,0},{16,8},{32,24},{48,40},{0,56},{9,17}... | collective-permute-start | bytes 98312 | tf_op jit(solution)/shard_map/ppermute | solution.py:306
  24.2 2.8 %collective-permute-start.1 = (f32[8,8,128]{2,1,0:T(8,128)S(1)}, f32[8,8,128]{2,1,0:T(8,128)S(1)}, u32[]{:S(2)}, u32[]{:S(2)}) collective-permute-start(f32[8,8,128]{2,1,0:T(8,128)S(1)} %all_to_all.15.field_ref.rhs_ref), channel_id=1, source_target_pairs={{0,8},{16,24},{32,40},{48,56},{8,0},{24,16},{40,32},{56,48},{1,9},... | collective-permute-start | bytes 98312 | tf_op jit(solution)/shard_map/ppermute | solution.py:306
  24.2 2.8 %collective-permute-start = (f32[8,8,128]{2,1,0:T(8,128)S(1)}, f32[8,8,128]{2,1,0:T(8,128)S(1)}, u32[]{:S(2)}, u32[]{:S(2)}) collective-permute-start(f32[8,8,128]{2,1,0:T(8,128)S(1)} %all_to_all.15.field_ref.rhs_ref), channel_id=1, source_target_pairs={{0,1},{2,3},{4,5},{6,7},{64,65},{66,67},{68,69},{70,71},{128,129},... | collective-permute-start | bytes 98312 | tf_op jit(solution)/shard_map/ppermute | solution.py:306
  27.6 5.5 %collective-permute-start.7 = (f32[8,8,128]{2,1,0:T(8,128)S(1)}, f32[8,8,128]{2,1,0:T(8,128)S(1)}, u32[]{:S(2)}, u32[]{:S(2)}) collective-permute-start(f32[8,8,128]{2,1,0:T(8,128)S(1)} %get-tuple-element.8.field_ref.image_ref), channel_id=1, source_target_pairs={{1,2},{3,4},{5,6},{7,64},{65,66},{67,68},{69,70},{71,128},{129,130... | collective-permute-start | bytes 98312 | tf_op jit(solution)/shard_map/ppermute | solution.py:306
  29.5 4.0 %collective-permute-start.6 = (f32[8,8,128]{2,1,0:T(8,128)S(1)}, f32[8,8,128]{2,1,0:T(8,128)S(1)}, u32[]{:S(2)}, u32[]{:S(2)}) collective-permute-start(f32[8,8,128]{2,1,0:T(8,128)S(1)} %get-tuple-element.8.field_ref.image_ref), channel_id=1, source_target_pairs={{8,16},{24,32},{40,48},{56,0},{16,8},{32,24},{48,40},{0,56},{9,17}... | collective-permute-start | bytes 98312 | tf_op jit(solution)/shard_map/ppermute | solution.py:306
  31.2 3.1 %collective-permute-start.5 = (f32[8,8,128]{2,1,0:T(8,128)S(1)}, f32[8,8,128]{2,1,0:T(8,128)S(1)}, u32[]{:S(2)}, u32[]{:S(2)}) collective-permute-start(f32[8,8,128]{2,1,0:T(8,128)S(1)} %get-tuple-element.8.field_ref.image_ref), channel_id=1, source_target_pairs={{0,8},{16,24},{32,40},{48,56},{8,0},{24,16},{40,32},{56,48},{1,9},... | collective-permute-start | bytes 98312 | tf_op jit(solution)/shard_map/ppermute | solution.py:306
  32.0 3.1 %collective-permute-start.4 = (f32[8,8,128]{2,1,0:T(8,128)S(1)}, f32[8,8,128]{2,1,0:T(8,128)S(1)}, u32[]{:S(2)}, u32[]{:S(2)}) collective-permute-start(f32[8,8,128]{2,1,0:T(8,128)S(1)} %get-tuple-element.8.field_ref.image_ref), channel_id=1, source_target_pairs={{0,1},{2,3},{4,5},{6,7},{64,65},{66,67},{68,69},{70,71},{128,129},... | collective-permute-start | bytes 98312 | tf_op jit(solution)/shard_map/ppermute | solution.py:306
  43.9 15.2 %all-to-all-start.2 = ((f32[32,1,128]{2,1,0:T(1,128)}), f32[32,1,128]{2,1,0:T(1,128)S(1)}, u32[]{:S(2)}, u32[]{:S(2)}) async-start(f32[32,1,128]{2,1,0:T(1,128)} %shard_map.55), calls=%async_computation.2 | async-start | bytes 32768 | tf_op jit(solution)/shard_map/all_to_all | solution.py:325
